TPU v7x, 32 devices: a whole 2x2x4 slice. The times are simulated.
32 devices in a mesh: section: 2 (over y), tensor: 2 (over x), dp: 8 (over z, core).
Axes of the slice: x: 2, y: 2, z: 4, core: 2. Of those that a mesh axis runs over, the one named last changes fastest.
Arguments:
- inputs: bfloat16 [2, 8192, 512], P(None, ('dp', 'tensor')), may hold values from -6 to 6
- cotangent: bfloat16 [2, 8192, 512], P(None, ('dp', 'tensor')), may hold values from -6 to 6
- lengths: int32 [2, 8], P(None, 'dp'), may hold values from 512 to 1024, as said below
- blocks: int32 [2, 8, 16, 3], P('section', 'tensor'), may hold values from 1 to 15
- feature_map: float32 [2, 8, 64, 256], P('section', 'tensor'), may hold values from -6 to 6
- w_qkv: bfloat16 [2, 512, 3, 512], P('section', None, None, 'tensor'), may hold values from -0.25 to 0.25
- b_qkv: bfloat16 [2, 3, 512], P('section', None, 'tensor'), may hold values from -4 to 4
- w_out: bfloat16 [2, 512, 512], P('section', 'tensor'), may hold values from -1 to 1
- w_up: bfloat16 [2, 512, 2048], P('section', None, 'tensor'), may hold values from -0.25 to 0.25
- b_up: bfloat16 [2, 2048], P('section', 'tensor'), may hold values from -4 to 4
- w_down: bfloat16 [2, 2048, 512], P('section', 'tensor'), may hold values from -0.125 to 0.125
- vector_params: bfloat16 [2, 6, 512], P('section'), may hold values from -4 to 4
Outputs:
- section_outputs: bfloat16 [2, 2, 8192, 512], P('section', None, ('dp', 'tensor'))
- input_grads: float32 [2, 2, 8192, 512], P('section', None, ('dp', 'tensor'))
- grad_qkv: float32 [2, 512, 3, 512], P('section', 'dp', None, 'tensor')
- grad_bqkv: float32 [2, 3, 512], P('section', None, ('tensor', 'dp'))
- grad_out: float32 [2, 512, 512], P('section', 'tensor', 'dp')
- grad_up: float32 [2, 512, 2048], P('section', 'dp', 'tensor')
- grad_bup: float32 [2, 2048], P('section', ('tensor', 'dp'))
- grad_down: float32 [2, 2048, 512], P('section', 'tensor', 'dp')
- grad_vectors: float32 [2, 6, 512], P('section', None, ('tensor', 'dp'))
Inputs may be any that keep to these rules, and one draw needn't show every extreme that they name: `lengths`: in each sequence group, one micro-batch's sequence has all 1024 tokens; the others may be shorter. Entries name key blocks other than block 0 and may repeat within a list.
All inputs are finite; a program needn't handle non-finite values.
Results may differ from a plain program's by a relative error of at most 0.04.
Values may be sent and summed in bfloat16 or wider, within the bound.
No kernel may reach another device: no remote copies, remote signals or barrier semaphores. Data moves between devices by JAX's collectives and lax.ppermute only.
A program may use at most 320 MiB of HBM per device.

v0:
```python
import jax
import jax.numpy as jnp
from jax import lax
from jax.sharding import PartitionSpec as P

HEAD = 64
BLOCK = 64
SEQ_LEN = 1024


norm_eps = 1e-05
bfloat = jnp.bfloat16
single = jnp.float32


def shifted(value, axis, steps):
    count = lax.axis_size(axis)
    first, last = (max(0, -steps), min(count, count - steps))
    return lax.ppermute(value, axis, [(source, source + steps) for source in range(first, last)])


def norm_rows(residual, gain_vec, shift_vec):
    row_mean = jnp.mean(residual, axis=-1, keepdims=True)
    centred = residual - row_mean
    variance = jnp.mean(centred * centred, axis=-1, keepdims=True)
    return centred * lax.rsqrt(variance + norm_eps) * (1.0 + gain_vec) + shift_vec


def gelu_exact(pre_active):
    return jax.nn.gelu(pre_active, approximate=False)


def select_tree(flag_value, when_true, when_false):
    return jax.tree.map(
        lambda left_arr, right_arr: jnp.where(flag_value, left_arr, right_arr),
        when_true,
        when_false,
    )


def split_pieces(operand):
    if operand.dtype == bfloat:
        return (operand,)
    upper_part = operand.astype(bfloat)
    lower_part = (operand - upper_part.astype(single)).astype(bfloat)
    return (upper_part, lower_part)


def split_dot(form, left, right):
    left_pieces = split_pieces(left)
    right_pieces = split_pieces(right)
    total = None
    for left_no, left_piece in enumerate(left_pieces):
        for right_no, right_piece in enumerate(right_pieces):
            if left_no + right_no > 1:
                continue
            term = jnp.einsum(form, left_piece, right_piece, preferred_element_type=single)
            total = term if total is None else total + term
    return total


def sparse_layout(block_list, length):
    head_count, block_count = (block_list.shape[0], block_list.shape[1])
    chosen = jnp.concatenate(
        [jnp.zeros((head_count, block_count, 1), jnp.int32), block_list], axis=2
    )
    key_live = (jnp.arange(SEQ_LEN) < length).astype(single)
    picked_live = key_live.reshape(block_count, BLOCK)[chosen].reshape(head_count, block_count, -1)
    return (chosen, key_live, picked_live)


def pick_blocks(table_in, chosen):
    head_count, block_count = (chosen.shape[0], chosen.shape[1])
    blocks_in = table_in.reshape(head_count, block_count, BLOCK, table_in.shape[-1])
    taken_rows = jax.vmap(lambda one_table, index_rows: one_table[index_rows])(blocks_in, chosen)
    return taken_rows.reshape(head_count, block_count, -1, table_in.shape[-1])


def place_blocks(values_in, chosen):
    head_count, block_count, slot_count = chosen.shape
    parts_in = values_in.reshape(head_count, block_count, slot_count, BLOCK, values_in.shape[-1])
    zero_blocks = jnp.zeros((head_count, block_count, BLOCK, values_in.shape[-1]), single)
    placed = jax.vmap(lambda base_arr, index_rows, one_part: base_arr.at[index_rows].add(one_part))(
        zero_blocks, chosen, parts_in
    )
    return placed.reshape(head_count, SEQ_LEN, values_in.shape[-1])


def feature_of(vectors_low, features):
    feature_scale = HEAD ** (-0.25)
    vectors = vectors_low.astype(single)
    projected = split_dot("hld,hdf->hlf", vectors_low, features) * feature_scale
    return jnp.exp(
        projected
        - jnp.sum(vectors * vectors, axis=-1, keepdims=True) * (0.5 * feature_scale * feature_scale)
    )


def block_scores(query_blocks, picked_keys, picked_live):
    scores = jnp.einsum(
        "hnqd,hnkd->hnqk", query_blocks, picked_keys, preferred_element_type=single
    ) * HEAD ** (-0.5)
    return jnp.where(picked_live[:, :, None, :] > 0.5, scores, -1e30)


def attend_forward(queries, key_vecs, value_vecs, chosen, key_live, picked_live, features):
    head_count, block_count = (chosen.shape[0], chosen.shape[1])
    query_blocks = queries.reshape(head_count, block_count, BLOCK, HEAD)
    picked_keys = pick_blocks(key_vecs, chosen)
    picked_values = pick_blocks(value_vecs, chosen)
    scores = block_scores(query_blocks, picked_keys, picked_live)
    row_max = jnp.max(scores, axis=-1, keepdims=True)
    weights_raw = jnp.exp(scores - row_max) * picked_live[:, :, None, :]
    row_total = jnp.sum(weights_raw, axis=-1, keepdims=True)
    log_total = row_max + jnp.log(row_total)
    weights_low = (weights_raw / row_total).astype(bfloat)
    sparse_out = jnp.einsum(
        "hnqk,hnkd->hnqd", weights_low, picked_values, preferred_element_type=single
    )
    sparse_out = sparse_out.reshape(head_count, SEQ_LEN, HEAD)
    query_feats = feature_of(queries, features)
    key_feats = feature_of(key_vecs, features) * key_live[None, :, None]
    moments = split_dot("hlf,hld->hfd", key_feats, value_vecs)
    totals = jnp.sum(key_feats, axis=1)
    numerator = split_dot("hlf,hfd->hld", query_feats, moments)
    denominator = split_dot("hlf,hf->hl", query_feats, totals)
    perf_out = numerator / denominator[:, :, None]
    return (
        sparse_out + perf_out,
        (log_total, query_feats, key_feats, moments, totals, denominator, perf_out),
    )


def attend_backward(
    grad_heads, queries, key_vecs, value_vecs, chosen, picked_live, features, attn_keep
):
    log_total, query_feats, key_feats, moments, totals, denominator, perf_out = attn_keep
    head_count, block_count = (chosen.shape[0], chosen.shape[1])
    score_scale = HEAD ** (-0.5)
    query_blocks = queries.reshape(head_count, block_count, BLOCK, HEAD)
    grad_blocks = grad_heads.reshape(head_count, block_count, BLOCK, HEAD)
    picked_keys = pick_blocks(key_vecs, chosen)
    picked_values = pick_blocks(value_vecs, chosen)
    scores = block_scores(query_blocks, picked_keys, picked_live)
    weights_f = jnp.exp(scores - log_total) * picked_live[:, :, None, :]
    grad_weights = jnp.einsum(
        "hnqd,hnkd->hnqk", grad_blocks, picked_values, preferred_element_type=single
    )
    row_inner = jnp.sum(weights_f * grad_weights, axis=-1, keepdims=True)
    grad_scores = (weights_f * (grad_weights - row_inner)).astype(bfloat)
    grad_query = jnp.einsum(
        "hnqk,hnkd->hnqd", grad_scores, picked_keys, preferred_element_type=single
    )
    grad_query = grad_query.reshape(head_count, SEQ_LEN, HEAD) * score_scale
    grad_keys = place_blocks(
        jnp.einsum("hnqk,hnqd->hnkd", grad_scores, query_blocks, preferred_element_type=single)
        * score_scale,
        chosen,
    )
    grad_values = place_blocks(
        jnp.einsum(
            "hnqk,hnqd->hnkd", weights_f.astype(bfloat), grad_blocks, preferred_element_type=single
        ),
        chosen,
    )
    grad_float = grad_heads.astype(single)
    grad_numer = grad_float / denominator[:, :, None]
    grad_denom = -jnp.sum(grad_float * perf_out, axis=-1) / denominator
    grad_qfeat = (
        split_dot("hld,hfd->hlf", grad_numer, moments) + grad_denom[:, :, None] * totals[:, None, :]
    )
    grad_moments = split_dot("hlf,hld->hfd", query_feats, grad_numer)
    grad_totals = split_dot("hlf,hl->hf", query_feats, grad_denom)
    grad_kfeat = split_dot("hld,hfd->hlf", value_vecs, grad_moments) + grad_totals[:, None, :]
    grad_values = grad_values + split_dot("hlf,hfd->hld", key_feats, grad_moments)
    feature_scale = HEAD ** (-0.25)

    def feature_back(grad_feat, feats, vectors_low):
        grad_expo = grad_feat * feats
        direct = split_dot("hlf,hdf->hld", grad_expo, features) * feature_scale
        return direct - feature_scale * feature_scale * jnp.sum(
            grad_expo, axis=-1, keepdims=True
        ) * vectors_low.astype(single)

    grad_query = grad_query + feature_back(grad_qfeat, query_feats, queries)
    grad_keys = grad_keys + feature_back(grad_kfeat, key_feats, key_vecs)
    return (grad_query, grad_keys, grad_values)


def layer_forward(section_entry, length, layer_params, block_list, features):
    qkv_mat, qkv_bias, out_mat, up_mat, up_bias, down_mat, vectors = layer_params
    residual = section_entry.astype(single)
    normed = norm_rows(residual, vectors[0], vectors[1]).astype(bfloat)
    normed_all = lax.all_gather(normed, "tensor", axis=0, tiled=True)
    projected = (
        jnp.einsum("ld,dce->lce", normed_all, qkv_mat, preferred_element_type=single)
        + qkv_bias[None]
    )
    projected = projected.astype(bfloat)
    seq_len, part_width = (projected.shape[0], projected.shape[2])
    head_count = part_width // HEAD
    head_parts = projected.reshape(seq_len, 3, head_count, HEAD).transpose(1, 2, 0, 3)
    chosen, key_live, picked_live = sparse_layout(block_list, length)
    mixed_heads, attn_keep = attend_forward(
        head_parts[0], head_parts[1], head_parts[2], chosen, key_live, picked_live, features
    )
    mixed_low = mixed_heads.transpose(1, 0, 2).reshape(seq_len, part_width).astype(bfloat)
    row_block = mixed_low
    branch = lax.psum_scatter(
        jnp.dot(row_block, out_mat, preferred_element_type=single).astype(jnp.bfloat16),
        "tensor",
        scatter_dimension=0,
        tiled=True,
    ).astype(jnp.float32)
    hidden_res = residual + branch + vectors[4]
    normed_two = norm_rows(hidden_res, vectors[2], vectors[3]).astype(bfloat)
    normed_two_all = lax.all_gather(normed_two, "tensor", axis=0, tiled=True)
    pre_active = jnp.dot(normed_two_all, up_mat, preferred_element_type=single) + up_bias
    active = gelu_exact(pre_active).astype(bfloat)
    row_block = active
    result = (
        hidden_res
        + lax.psum_scatter(
            jnp.dot(row_block, down_mat, preferred_element_type=single).astype(jnp.bfloat16),
            "tensor",
            scatter_dimension=0,
            tiled=True,
        ).astype(jnp.float32)
        + vectors[5]
    )
    record = (
        residual,
        hidden_res,
        normed_all,
        head_parts,
        mixed_low,
        normed_two_all,
        pre_active,
        active,
        attn_keep,
        length,
    )
    return (result.astype(bfloat), record)


def layer_backward(grad_low, record, layer_params, block_list, features):
    qkv_mat, qkv_bias, out_mat, up_mat, up_bias, down_mat, vectors = layer_params
    (
        residual,
        hidden_res,
        normed_all,
        head_parts,
        mixed_low,
        normed_two_all,
        pre_active,
        active,
        attn_keep,
        length,
    ) = record
    seq_len, part_width = mixed_low.shape
    head_count = part_width // HEAD
    grad_output = grad_low.astype(single)
    grad_all = lax.all_gather(grad_low, "tensor", axis=0, tiled=True)
    grad_wdown = jnp.einsum("lf,ld->fd", active, grad_all, preferred_element_type=single)
    grad_active = jnp.einsum("ld,fd->lf", grad_all, down_mat, preferred_element_type=single)
    _, gelu_pull = jax.vjp(gelu_exact, pre_active)
    grad_upper = gelu_pull(grad_active)[0].astype(bfloat)
    grad_wup = jnp.einsum("ld,lf->df", normed_two_all, grad_upper, preferred_element_type=single)
    grad_bup = jnp.sum(grad_upper.astype(single), axis=0)
    row_block = grad_upper
    grad_normed_two = lax.psum_scatter(
        jnp.einsum("lf,df->ld", row_block, up_mat, preferred_element_type=single).astype(
            jnp.bfloat16
        ),
        "tensor",
        scatter_dimension=0,
        tiled=True,
    ).astype(jnp.float32)
    _, pull_two = jax.vjp(norm_rows, hidden_res, vectors[2], vectors[3])
    grad_hidden, grad_gain_two, grad_shift_two = pull_two(grad_normed_two)
    grad_hidden = grad_hidden + grad_output
    grad_hidden_low = grad_hidden.astype(bfloat)
    hidden_all = lax.all_gather(grad_hidden_low, "tensor", axis=0, tiled=True)
    grad_wout = jnp.einsum("le,ld->ed", mixed_low, hidden_all, preferred_element_type=single)
    grad_mixed = jnp.einsum("ld,ed->le", hidden_all, out_mat, preferred_element_type=single).astype(
        bfloat
    )
    grad_heads = grad_mixed.reshape(seq_len, head_count, HEAD).transpose(1, 0, 2)
    chosen, key_live, picked_live = sparse_layout(block_list, length)
    grad_query, grad_keys, grad_values = attend_backward(
        grad_heads,
        head_parts[0],
        head_parts[1],
        head_parts[2],
        chosen,
        picked_live,
        features,
        attn_keep,
    )
    grad_proj = (
        jnp.stack([grad_query, grad_keys, grad_values])
        .transpose(2, 0, 1, 3)
        .reshape(seq_len, 3, part_width)
        .astype(bfloat)
    )
    grad_wqkv = jnp.einsum("ld,lce->dce", normed_all, grad_proj, preferred_element_type=single)
    grad_bqkv = jnp.sum(grad_proj.astype(single), axis=0)
    row_block = grad_proj
    grad_normed = lax.psum_scatter(
        jnp.einsum("lce,dce->ld", row_block, qkv_mat, preferred_element_type=single).astype(
            jnp.bfloat16
        ),
        "tensor",
        scatter_dimension=0,
        tiled=True,
    ).astype(jnp.float32)
    _, pull_one = jax.vjp(norm_rows, residual, vectors[0], vectors[1])
    grad_resid, grad_gain_one, grad_shift_one = pull_one(grad_normed)
    grad_resid = grad_resid + grad_hidden
    weight_grads = (grad_wqkv, grad_bqkv, grad_wout, grad_wup, grad_bup, grad_wdown)
    vector_grads = jnp.stack(
        [
            grad_gain_one,
            grad_shift_one,
            grad_gain_two,
            grad_shift_two,
            jnp.sum(grad_hidden_low.astype(single), axis=0),
            jnp.sum(grad_output, axis=0),
        ]
    )
    return (grad_resid, weight_grads, vector_grads)


def shards(
    inputs,
    cotangent,
    lengths,
    blocks,
    feature_map,
    w_qkv,
    b_qkv,
    w_out,
    w_up,
    b_up,
    w_down,
    vector_params,
):
    section_no = lax.axis_index("section")
    is_first = section_no == 0
    is_last = section_no == lax.axis_size("section") - 1
    layer_params = (
        w_qkv[0],
        b_qkv[0].astype(single),
        w_out[0],
        w_up[0],
        b_up[0].astype(single),
        w_down[0],
        vector_params[0].astype(single),
    )
    block_list = blocks[0]
    features = feature_map[0]
    batch_count = inputs.shape[0]
    carried = jnp.zeros_like(inputs[0])
    records = []
    results = []
    for tick_no in range(batch_count + 1):
        batch_no = jnp.clip(tick_no - section_no, 0, batch_count - 1)
        section_entry = jnp.where(is_first, inputs[min(tick_no, batch_count - 1)], carried)
        result, record = layer_forward(
            section_entry, lengths[batch_no, 0], layer_params, block_list, features
        )
        records.append(record)
        results.append(result)
        if tick_no < batch_count:
            carried = shifted(result, "section", 1)
    section_outputs = jnp.stack(
        [
            jnp.where(is_first, results[batch_idx], results[batch_idx + 1])
            for batch_idx in range(batch_count)
        ]
    )[None]
    received = jnp.zeros_like(cotangent[0])
    grad_list = []
    local_sum = None
    vector_total = jnp.zeros((6, inputs.shape[2]), single)
    for tick_no in range(batch_count + 1):
        record = select_tree(
            is_last, records[min(tick_no + 1, batch_count)], records[max(tick_no - 1, 0)]
        )
        valid_flag = jnp.where(is_last, float(tick_no < batch_count), float(tick_no >= 1)).astype(
            single
        )
        grad_entry = jnp.where(is_last, cotangent[min(tick_no, batch_count - 1)], received)
        grad_resid, weight_grads, vector_grads = layer_backward(
            grad_entry, record, layer_params, block_list, features
        )
        weight_grads = tuple((valid_flag * addend for addend in weight_grads))
        vector_total = vector_total + valid_flag * vector_grads
        local_sum = (
            weight_grads
            if local_sum is None
            else tuple((summed + addend for summed, addend in zip(local_sum, weight_grads)))
        )
        grad_list.append(grad_resid)
        if tick_no < batch_count:
            received = shifted(grad_resid.astype(bfloat), "section", -1)
    final_grads = (
        lax.psum_scatter(
            local_sum[0].astype(jnp.bfloat16), "dp", scatter_dimension=0, tiled=True
        ).astype(jnp.float32),
        lax.psum_scatter(
            local_sum[1].astype(jnp.bfloat16), "dp", scatter_dimension=1, tiled=True
        ).astype(jnp.float32),
        lax.psum_scatter(
            local_sum[2].astype(jnp.bfloat16), "dp", scatter_dimension=1, tiled=True
        ).astype(jnp.float32),
        lax.psum_scatter(
            local_sum[3].astype(jnp.bfloat16), "dp", scatter_dimension=0, tiled=True
        ).astype(jnp.float32),
        lax.psum_scatter(
            local_sum[4].astype(jnp.bfloat16), "dp", scatter_dimension=0, tiled=True
        ).astype(jnp.float32),
        lax.psum_scatter(
            local_sum[5].astype(jnp.bfloat16), "dp", scatter_dimension=1, tiled=True
        ).astype(jnp.float32),
    )
    input_grads = jnp.stack(
        [
            jnp.where(is_first, grad_list[batch_idx + 1], grad_list[batch_idx])
            for batch_idx in range(batch_count)
        ]
    )[None]
    grad_vectors = lax.psum_scatter(
        vector_total, ("tensor", "dp"), scatter_dimension=1, tiled=True
    )[None]
    grad_wqkv, grad_bqkv, grad_wout, grad_wup, grad_bup, grad_wdown = final_grads
    return (
        section_outputs,
        input_grads,
        grad_wqkv[None],
        grad_bqkv[None],
        grad_wout[None],
        grad_wup[None],
        grad_bup[None],
        grad_wdown[None],
        grad_vectors,
    )


def solution(mesh):
    placed = (
        P(None, ("dp", "tensor"), None),
        P(None, ("dp", "tensor"), None),
        P(None, "dp"),
        P("section", "tensor", None, None),
        P("section", "tensor", None, None),
        P("section", None, None, "tensor"),
        P("section", None, "tensor"),
        P("section", "tensor", None),
        P("section", None, "tensor"),
        P("section", "tensor"),
        P("section", "tensor", None),
        P("section", None, None),
    )
    return jax.shard_map(
        shards,
        mesh=mesh,
        in_specs=placed,
        out_specs=(
            P("section", None, ("dp", "tensor"), None),
            P("section", None, ("dp", "tensor"), None),
            P("section", "dp", None, "tensor"),
            P("section", None, ("tensor", "dp")),
            P("section", "tensor", "dp"),
            P("section", "dp", "tensor"),
            P("section", ("tensor", "dp")),
            P("section", "tensor", "dp"),
            P("section", None, ("tensor", "dp")),
        ),
        check_vma=False,
    )
```

profile of v0, /device:TPU:0, one launch (start us, length us, event | category | flops | bytes accessed | tf_op | source)
XLA Modules:
  0.0 1454.3 jit_solution(8560657372094553003)
XLA Ops:
  20.2 18.1 %all-gather.14.cloned.1.call-done = bf16[1024,512]{1,0:T(8,128)(2,1)} async-done(((bf16[512,512]{1,0:T(8,128)(2,1)}), bf16[1024,512]{1,0:T(8,128)(2,1)}) %all-gather.14.cloned.1.call-update) | async-done | bytes 1048592 | tf_op jit(solution)/shard_map/all_gather | solution.py:194
  89.6 20.4 %reduce-scatter.23.cloned.1.call-done = bf16[512,512]{1,0:T(8,128)(2,1)} async-done(((bf16[1024,512]{1,0:T(8,128)(2,1)}), bf16[512,512]{1,0:T(8,128)(2,1)}) %reduce-scatter.23.cloned.1.call-update) | async-done | bytes 524304 | tf_op jit(solution)/shard_map/reduce_scatter | solution.py:209
  115.1 21.4 %all-gather.16.cloned.1.call-done = bf16[1024,512]{1,0:T(8,128)(2,1)} async-done(((bf16[512,512]{1,0:T(8,128)(2,1)}), bf16[1024,512]{1,0:T(8,128)(2,1)}) %all-gather.16.cloned.1.call-update) | async-done | bytes 1048592 | tf_op jit(solution)/shard_map/all_gather | solution.py:217
  152.3 20.4 %reduce-scatter.25.cloned.1.call-done = bf16[512,512]{1,0:T(8,128)(2,1)} async-done(((bf16[1024,512]{1,0:T(8,128)(2,1)}), bf16[512,512]{1,0:T(8,128)(2,1)}) %reduce-scatter.25.cloned.1.call-update) | async-done | bytes 524304 | tf_op jit(solution)/shard_map/reduce_scatter | solution.py:223
  192.8 19.9 %all-gather.18.cloned.1.call-done = bf16[1024,512]{1,0:T(8,128)(2,1)} async-done(((bf16[512,512]{1,0:T(8,128)(2,1)}), bf16[1024,512]{1,0:T(8,128)(2,1)}) %all-gather.18.cloned.1.call-update) | async-done | bytes 1048592 | tf_op jit(solution)/shard_map/all_gather | solution.py:194
  267.1 20.4 %reduce-scatter.27.cloned.1.call-done = bf16[512,512]{1,0:T(8,128)(2,1)} async-done(((bf16[1024,512]{1,0:T(8,128)(2,1)}), bf16[512,512]{1,0:T(8,128)(2,1)}) %reduce-scatter.27.cloned.1.call-update) | async-done | bytes 524304 | tf_op jit(solution)/shard_map/reduce_scatter | solution.py:209
  295.9 18.8 %all-gather.20.cloned.1.call-done = bf16[1024,512]{1,0:T(8,128)(2,1)} async-done(((bf16[512,512]{1,0:T(8,128)(2,1)}), bf16[1024,512]{1,0:T(8,128)(2,1)}) %all-gather.20.cloned.1.call-update) | async-done | bytes 1048592 | tf_op jit(solution)/shard_map/all_gather | solution.py:217
  337.6 14.1 convert_reduce_fusion.2
  367.1 15.7 %reduce-scatter.35.cloned.1.call-done = bf16[512,512]{1,0:T(8,128)(2,1)} async-done(((bf16[1024,512]{1,0:T(8,128)(2,1)}), bf16[512,512]{1,0:T(8,128)(2,1)}) %reduce-scatter.35.cloned.1.call-update) | async-done | bytes 524304 | tf_op jit(solution)/shard_map/reduce_scatter | solution.py:271
  394.8 17.3 %all-gather.26.cloned.1.call-done = bf16[1024,512]{1,0:T(8,128)(2,1)} async-done(((bf16[512,512]{1,0:T(8,128)(2,1)}), bf16[1024,512]{1,0:T(8,128)(2,1)}) %all-gather.26.cloned.1.call-update) | async-done | bytes 1048592 | tf_op jit(solution)/shard_map/all_gather | solution.py:283
  417.8 17.7 %all-gather.22.cloned.1.call-done = bf16[1024,512]{1,0:T(8,128)(2,1)} async-done(((bf16[512,512]{1,0:T(8,128)(2,1)}), bf16[1024,512]{1,0:T(8,128)(2,1)}) %all-gather.22.cloned.1.call-update) | async-done | bytes 1048592 | tf_op jit(solution)/shard_map/all_gather | solution.py:194
  562.6 41.4 %scatter_fusion.1 = f32[4,16,64,64]{3,2,1,0:T(8,128)} fusion(f32[4,16,64,64]{3,2,1,0:T(8,128)} %broadcast.681.clone, s32[256]{0:T(256)S(1)} %reshape.864, f32[256,64,64]{2,1,0:T(8,128)} %bitcast.746), kind=kCustom, calls=%fused_computation.19 | custom fusion | flops 1048576 | bytes 12584960 | tf_op jit(solution)/shard_map/vmap()/scatter-add | solution.py:83
  634.0 40.8 %scatter_fusion = f32[4,16,64,64]{3,2,1,0:T(8,128)} fusion(f32[4,16,64,64]{3,2,1,0:T(8,128)} %broadcast.681.clone.1, s32[256]{0:T(256)S(1)} %reshape.864, f32[256,64,64]{2,1,0:T(8,128)} %bitcast.744), kind=kCustom, calls=%fused_computation.18 | custom fusion | flops 1048576 | bytes 12584960 | tf_op jit(solution)/shard_map/vmap()/scatter-add | solution.py:83
  695.9 18.6 %reduce-scatter.37.cloned.1.call-done = bf16[512,512]{1,0:T(8,128)(2,1)} async-done(((bf16[1024,512]{1,0:T(8,128)(2,1)}), bf16[512,512]{1,0:T(8,128)(2,1)}) %reduce-scatter.37.cloned.1.call-update) | async-done | bytes 524304 | tf_op jit(solution)/shard_map/reduce_scatter | solution.py:309
  726.9 14.3 collective-permute-done.2
  743.8 12.3 fusion.8
  766.6 13.5 convert_reduce_fusion.1
  784.2 19.9 %reduce-scatter.39.cloned.1.call-done = bf16[512,512]{1,0:T(8,128)(2,1)} async-done(((bf16[1024,512]{1,0:T(8,128)(2,1)}), bf16[512,512]{1,0:T(8,128)(2,1)}) %reduce-scatter.39.cloned.1.call-update) | async-done | bytes 524304 | tf_op jit(solution)/shard_map/reduce_scatter | solution.py:271
  866.7 28.0 %scatter_fusion.3 = f32[4,16,64,64]{3,2,1,0:T(8,128)S(1)} fusion(f32[4,16,64,64]{3,2,1,0:T(8,128)S(1)} %broadcast.681.clone.2, s32[256]{0:T(256)S(1)} %reshape.864, f32[256,64,64]{2,1,0:T(8,128)} %bitcast.748), kind=kCustom, calls=%fused_computation.21 | custom fusion | flops 1048576 | bytes 12584960 | tf_op jit(solution)/shard_map/vmap()/scatter-add | solution.py:83
  914.3 28.2 %scatter_fusion.2 = f32[4,16,64,64]{3,2,1,0:T(8,128)S(1)} fusion(f32[4,16,64,64]{3,2,1,0:T(8,128)S(1)} %broadcast.681.clone.3, s32[256]{0:T(256)S(1)} %reshape.864, f32[256,64,64]{2,1,0:T(8,128)} %bitcast.745), kind=kCustom, calls=%fused_computation.20 | custom fusion | flops 1048576 | bytes 12584960 | tf_op jit(solution)/shard_map/vmap()/scatter-add | solution.py:83
  973.5 20.4 %reduce-scatter.41.cloned.1.call-done = bf16[512,512]{1,0:T(8,128)(2,1)} async-done(((bf16[1024,512]{1,0:T(8,128)(2,1)}), bf16[512,512]{1,0:T(8,128)(2,1)}) %reduce-scatter.41.cloned.1.call-update) | async-done | bytes 524304 | tf_op jit(solution)/shard_map/reduce_scatter | solution.py:309
  1004.0 14.3 collective-permute-done.3
  1019.9 20.5 %all-gather.32.cloned.1.call-done = bf16[1024,512]{1,0:T(8,128)(2,1)} async-done(((bf16[512,512]{1,0:T(8,128)(2,1)}), bf16[1024,512]{1,0:T(8,128)(2,1)}) %all-gather.32.cloned.1.call-update) | async-done | bytes 1048592 | tf_op jit(solution)/shard_map/all_gather | solution.py:263
  1040.4 14.1 convert_reduce_fusion
  1058.5 20.1 %reduce-scatter.43.cloned.1.call-done = bf16[512,512]{1,0:T(8,128)(2,1)} async-done(((bf16[1024,512]{1,0:T(8,128)(2,1)}), bf16[512,512]{1,0:T(8,128)(2,1)}) %reduce-scatter.43.cloned.1.call-update) | async-done | bytes 524304 | tf_op jit(solution)/shard_map/reduce_scatter | solution.py:271
  1163.0 28.0 %scatter_fusion.5 = f32[4,16,64,64]{3,2,1,0:T(8,128)S(1)} fusion(f32[4,16,64,64]{3,2,1,0:T(8,128)S(1)} %broadcast.681.clone.4, s32[256]{0:T(256)S(1)} %reshape.864, f32[256,64,64]{2,1,0:T(8,128)} %bitcast.747), kind=kCustom, calls=%fused_computation.23 | custom fusion | flops 1048576 | bytes 12584960 | tf_op jit(solution)/shard_map/vmap()/scatter-add | solution.py:83
  1211.2 28.2 %scatter_fusion.4 = f32[4,16,64,64]{3,2,1,0:T(8,128)S(1)} fusion(f32[4,16,64,64]{3,2,1,0:T(8,128)S(1)} %broadcast.681.clone.5, s32[256]{0:T(256)S(1)} %reshape.864, f32[256,64,64]{2,1,0:T(8,128)} %bitcast.743), kind=kCustom, calls=%fused_computation.22 | custom fusion | flops 1048576 | bytes 12584960 | tf_op jit(solution)/shard_map/vmap()/scatter-add | solution.py:83
  1290.0 16.8 %all-reduce.1 = bf16[1024]{0:T(1024)(128)(2,1)S(1)} all-reduce(bf16[1024]{0:T(1024)(128)(2,1)S(1)} %add_convert_fusion.16), channel_id=19, replica_groups=mesh['section'=2,'tensor'=2,'dp'=8] {'dp'}, use_global_device_ids=true, to_apply=%region_91.92.clone | all-reduce | flops 1024 | bytes 4096
  1312.0 21.0 %reduce-scatter.49.cloned.1.call-done = bf16[256,64]{0,1:T(8,128)(2,1)} async-done(((bf16[256,512]{0,1:T(8,128)(2,1)}), bf16[256,64]{0,1:T(8,128)(2,1)}) %reduce-scatter.49.cloned.1.call-update) | async-done | bytes 32784 | tf_op jit(solution)/shard_map/reduce_scatter | solution.py:414
  1334.3 30.8 %reduce-scatter.47.cloned.1.call-done = bf16[64,3,256]{2,0,1:T(8,128)(2,1)} async-done(((bf16[512,3,256]{2,0,1:T(8,128)(2,1)}), bf16[64,3,256]{2,0,1:T(8,128)(2,1)}) %reduce-scatter.47.cloned.1.call-update) | async-done | bytes 98320 | tf_op jit(solution)/shard_map/reduce_scatter | solution.py:408
  1366.7 19.3 %reduce-scatter.45.cloned.1.call-done = bf16[512,512]{1,0:T(8,128)(2,1)} async-done(((bf16[1024,512]{1,0:T(8,128)(2,1)}), bf16[512,512]{1,0:T(8,128)(2,1)}) %reduce-scatter.45.cloned.1.call-update) | async-done | bytes 524304 | tf_op jit(solution)/shard_map/reduce_scatter | solution.py:309
  1394.0 51.8 %reduce-scatter.57.cloned.1.call-done = f32[32,6]{1,0:T(8,128)} async-done(((f32[512,6]{1,0:T(8,128)}), f32[32,6]{1,0:T(8,128)}) %reduce-scatter.57.cloned.1.call-update) | async-done | bytes 784
  (1028 shorter events, 725.6 us)
Async XLA Ops:
  7.2 31.1 %all-gather.14.cloned.1.call-start = ((), (), s32[]{:S(2)}) async-start(), calls=%async_computation.18 | async-start | bytes 1572864 | tf_op jit(solution)/shard_map/all_gather | solution.py:194
  14.1 95.9 %reduce-scatter.23.cloned.1.call-start = ((), (), s32[]{:S(2)}) async-start(), calls=%async_computation.19 | async-start | bytes 1572864 | tf_op jit(solution)/shard_map/reduce_scatter | solution.py:209
  89.5 46.9 %all-gather.16.cloned.1.call-start = ((), (), s32[]{:S(2)}) async-start(), calls=%async_computation.20 | async-start | bytes 1572864 | tf_op jit(solution)/shard_map/all_gather | solution.py:217
  115.0 57.7 %reduce-scatter.25.cloned.1.call-start = ((), (), s32[]{:S(2)}) async-start(), calls=%async_computation.21 | async-start | bytes 1572864 | tf_op jit(solution)/shard_map/reduce_scatter | solution.py:223
  152.2 60.5 %all-gather.18.cloned.1.call-start = ((), (), s32[]{:S(2)}) async-start(), calls=%async_computation.22 | async-start | bytes 1572864 | tf_op jit(solution)/shard_map/all_gather | solution.py:194
  190.2 97.3 %reduce-scatter.27.cloned.1.call-start = ((), (), s32[]{:S(2)}) async-start(), calls=%async_computation.23 | async-start | bytes 1572864 | tf_op jit(solution)/shard_map/reduce_scatter | solution.py:209
  267.0 47.6 %all-gather.20.cloned.1.call-start = ((), (), s32[]{:S(2)}) async-start(), calls=%async_computation.24 | async-start | bytes 1572864 | tf_op jit(solution)/shard_map/all_gather | solution.py:217
  293.2 44.4 %all-gather.36.cloned.1.call-start = ((), (), s32[]{:S(2)}) async-start(), calls=%async_computation.45 | async-start | bytes 1572864 | tf_op jit(solution)/shard_map/all_gather | solution.py:263
  295.9 64.5 %reduce-scatter.29.cloned.1.call-start = ((), (), s32[]{:S(2)}) async-start(), calls=%async_computation.25 | async-start | bytes 1572864 | tf_op jit(solution)/shard_map/reduce_scatter | solution.py:223
  330.5 52.3 %reduce-scatter.35.cloned.1.call-start = ((), (), s32[]{:S(2)}) async-start(), calls=%async_computation.30 | async-start | bytes 1572864 | tf_op jit(solution)/shard_map/reduce_scatter | solution.py:271
  355.4 56.7 %all-gather.26.cloned.1.call-start = ((), (), s32[]{:S(2)}) async-start(), calls=%async_computation.31 | async-start | bytes 1572864 | tf_op jit(solution)/shard_map/all_gather | solution.py:283
  363.1 27.6 %collective-permute-start.1 = (bf16[512,512]{1,0:T(8,128)(2,1)}, bf16[512,512]{1,0:T(8,128)(2,1)}, u32[]{:S(2)}, u32[]{:S(2)}) collective-permute-start(bf16[512,512]{1,0:T(8,128)(2,1)} %get-tuple-element.112), channel_id=1, source_target_pairs={{0,16},{1,17},{2,18},{3,19},{4,20},{5,21},{6,22},{7,23},{8,24},{9,... | collective-permute-start | bytes 1572872 | tf_op jit(solution)/shard_map/ppermute | solution.py:19
  390.6 44.9 %all-gather.22.cloned.1.call-start = ((), (), s32[]{:S(2)}) async-start(), calls=%async_computation.26 | async-start | bytes 1572864 | tf_op jit(solution)/shard_map/all_gather | solution.py:194
  392.4 302.2 %reduce-scatter.31.cloned.1.call-start = ((), (), s32[]{:S(2)}) async-start(), calls=%async_computation.27 | async-start | bytes 1572864 | tf_op jit(solution)/shard_map/reduce_scatter | solution.py:209
  560.9 153.6 %reduce-scatter.37.cloned.1.call-start = ((), (), s32[]{:S(2)}) async-start(), calls=%async_computation.32 | async-start | bytes 1572864 | tf_op jit(solution)/shard_map/reduce_scatter | solution.py:309
  694.3 49.5 %all-gather.24.cloned.1.call-start = ((), (), s32[]{:S(2)}) async-start(), calls=%async_computation.28 | async-start | bytes 1572864 | tf_op jit(solution)/shard_map/all_gather | solution.py:217
  722.3 44.3 %all-gather.28.cloned.1.call-start = ((), (), s32[]{:S(2)}) async-start(), calls=%async_computation.33 | async-start | bytes 1572864 | tf_op jit(solution)/shard_map/all_gather | solution.py:263
  742.7 61.4 %reduce-scatter.39.cloned.1.call-start = ((), (), s32[]{:S(2)}) async-start(), calls=%async_computation.34 | async-start | bytes 1572864 | tf_op jit(solution)/shard_map/reduce_scatter | solution.py:271
  783.7 48.8 %all-gather.30.cloned.1.call-start = ((), (), s32[]{:S(2)}) async-start(), calls=%async_computation.35 | async-start | bytes 1572864 | tf_op jit(solution)/shard_map/all_gather | solution.py:283
  811.0 182.8 %reduce-scatter.41.cloned.1.call-start = ((), (), s32[]{:S(2)}) async-start(), calls=%async_computation.36 | async-start | bytes 1572864 | tf_op jit(solution)/shard_map/reduce_scatter | solution.py:309
  973.4 67.0 %all-gather.32.cloned.1.call-start = ((), (), s32[]{:S(2)}) async-start(), calls=%async_computation.37 | async-start | bytes 1572864 | tf_op jit(solution)/shard_map/all_gather | solution.py:263
  1002.7 15.6 %collective-permute-start.3 = (bf16[512,512]{1,0:T(8,128)(2,1)S(1)}, bf16[512,512]{1,0:T(8,128)(2,1)S(1)}, u32[]{:S(2)}, u32[]{:S(2)}) collective-permute-start(bf16[512,512]{1,0:T(8,128)(2,1)S(1)} %convert_element_type.1022), channel_id=1, source_target_pairs={{16,0},{17,1},{18,2},{19,3},{20,4},{21,5},{22,6},{23,7},{24,8},{25... | collective-permute-start | bytes 1572872 | tf_op jit(solution)/shard_map/ppermute | solution.py:19
  1019.8 58.7 %reduce-scatter.43.cloned.1.call-start = ((), (), s32[]{:S(2)}) async-start(), calls=%async_computation.38 | async-start | bytes 1572864 | tf_op jit(solution)/shard_map/reduce_scatter | solution.py:271
  1058.1 70.9 %all-gather.34.cloned.1.call-start = ((), (), s32[]{:S(2)}) async-start(), calls=%async_computation.39 | async-start | bytes 1572864 | tf_op jit(solution)/shard_map/all_gather | solution.py:283
  1084.8 201.2 %reduce-scatter.33.cloned.1.call-start = ((), (), s32[]{:S(2)}) async-start(), calls=%async_computation.29 | async-start | bytes 1572864 | tf_op jit(solution)/shard_map/reduce_scatter | solution.py:223
  1090.3 217.0 %reduce-scatter.51.cloned.1.call-start = ((), (), s32[]{:S(2)}) async-start(), calls=%async_computation.43 | async-start | bytes 1179648 | tf_op jit(solution)/shard_map/reduce_scatter | solution.py:417
  1102.8 206.2 %reduce-scatter.53.cloned.1.call-start = ((), (), s32[]{:S(2)}) async-start(), calls=%async_computation.44 | async-start | bytes 1179648 | tf_op jit(solution)/shard_map/reduce_scatter | solution.py:423
  1128.9 181.7 %reduce-scatter.55.cloned.1.call-start = ((), (), s32[]{:S(2)}) async-start(), calls=%async_computation.46 | async-start | bytes 73728
  1270.8 62.1 %reduce-scatter.49.cloned.1.call-start = ((), (), s32[]{:S(2)}) async-start(), calls=%async_computation.42 | async-start | bytes 294912 | tf_op jit(solution)/shard_map/reduce_scatter | solution.py:414
  1275.6 89.5 %reduce-scatter.47.cloned.1.call-start = ((), (), s32[]{:S(2)}) async-start(), calls=%async_computation.41 | async-start | bytes 884736 | tf_op jit(solution)/shard_map/reduce_scatter | solution.py:408
  1280.8 105.2 %reduce-scatter.45.cloned.1.call-start = ((), (), s32[]{:S(2)}) async-start(), calls=%async_computation.40 | async-start | bytes 1572864 | tf_op jit(solution)/shard_map/reduce_scatter | solution.py:309
  1285.9 159.9 %reduce-scatter.57.cloned.1.call-start = ((), (), s32[]{:S(2)}) async-start(), calls=%async_computation.47 | async-start | bytes 278528
  (282 other events, 7914.8 us)
Sparse Core Ops, SparseCore 0:
  14.2 23.9 all-gather.13
  89.7 20.3 reduce-scatter.22
  115.1 21.2 all-gather.15
  152.3 20.3 reduce-scatter.24
  190.4 22.3 all-gather.17
  267.2 20.3 reduce-scatter.26
  293.3 21.2 all-gather.19
  316.3 21.2 all-gather.35
  340.0 20.3 reduce-scatter.28
  362.4 20.3 reduce-scatter.34
  390.8 21.2 all-gather.25
  414.2 21.2 all-gather.21
  561.1 20.3 reduce-scatter.30
  694.4 20.0 reduce-scatter.36
  722.4 21.3 all-gather.23
  745.3 21.2 all-gather.27
  783.8 20.3 reduce-scatter.38
  811.1 21.3 all-gather.29
  973.5 20.2 reduce-scatter.40
  1020.0 20.3 all-gather.31
  1058.2 20.3 reduce-scatter.42
  1085.0 21.2 all-gather.33
  1109.1 20.3 reduce-scatter.32
  1131.7 32.3 reduce-scatter.50
  1166.5 30.6 reduce-scatter.52
  1271.0 31.4 reduce-scatter.54
  1304.5 28.3 reduce-scatter.48
  1335.3 29.7 reduce-scatter.46
  1367.4 18.5 reduce-scatter.44
  1390.4 55.3 reduce-scatter.56
where the time goes:
time: 1470 us; the launch traced here: 1450 us
  waiting for transfers between devices  480 us (33%)
  matrix products  396 us (27%)
  other arithmetic  302 us (21%)
  local copies, waits for them, and re-layouts  225 us (15%)
  between operations  22.4 us (2%)
  blocking collectives  16.8 us (1%)
    scatter-add x6, other arithmetic, place_blocks(): base_arr.at[index_rows].add(one_part)  195 us
    dot_general x96, matrix products, split_dot(): jnp.einsum(form, left_piece, right_piece, preferred_element_type=single)  167 us
    unnamed x567, local copies, waits for them, and re-layouts  59.2 us
    reduce_scatter x3, waiting for transfers between devices, layer_backward(): lax.psum_scatter(jnp.einsum('lce,dce->ld', row_block, qkv_mat, preferred_...  58.3 us
    reduce_scatter x3, waiting for transfers between devices, layer_backward(): lax.psum_scatter(jnp.einsum('lf,df->ld', row_block, up_mat, preferred_ele...  55.7 us
    all_gather x3, waiting for transfers between devices, layer_forward(): normed_all = lax.all_gather(normed, 'tensor', axis=0, tiled=True)  55.7 us
    unnamed x32, waiting for transfers between devices  52.3 us
    gather x16, local copies, waits for them, and re-layouts, pick_blocks(): one_table[index_rows]  51.1 us
  transfers between devices with their start and end apart: 34, of which 27 were waited for; matrix products, arithmetic and copies ran while one was open for 29% of the time, Pallas kernels for 0%

commit v1 on v0

--- a/solution.py
+++ b/solution.py
@@ -1,7 +1,1008 @@
+import functools
+
 import jax
 import jax.numpy as jnp
 from jax import lax
+from jax.experimental import pallas as pl
+from jax.experimental.pallas import tpu as pltpu
 from jax.sharding import PartitionSpec as P
+
+HEAD = 64
+BLOCK = 64
+NORM_EPS = 1e-5
+bf = jnp.bfloat16
+f32 = jnp.float32
+LOG2E = 1.4426950408889634
+F_SCALE = HEAD ** -0.25
+ROWS = 256
+VMEM_BYTES = 60 * 1024 * 1024
+ANY = pl.BlockSpec(memory_space=pl.ANY)
+WHOLE = pl.BlockSpec(memory_space=pltpu.VMEM)
+SCALARS = pl.BlockSpec(memory_space=pltpu.SMEM)
+
+
+def contract(left, right, left_dim, right_dim):
+    return lax.dot_general(
+        left, right, (((left_dim,), (right_dim,)), ((), ())), preferred_element_type=f32
+    )
+
+
+def pick_source(layer_no):
+    section_no = lax.axis_index("section")
+    same = lax.rem(lax.axis_index("dp"), 2) == lax.axis_index("tensor")
+    return jnp.where(
+        section_no == layer_no, jnp.where(same, 0, 1), jnp.where(same, 1, 2)
+    )
+
+
+def start_pick(source, candidates, target, sem):
+    for number, candidate in enumerate(candidates):
+
+        @pl.when(source == number)
+        def _():
+            pltpu.make_async_copy(candidate, target, sem).start()
+
+
+def wait_pick(candidates, target, sem):
+    pltpu.make_async_copy(candidates[0], target, sem).wait()
+
+
+def small_row(small, row, width):
+    return small[row : row + 1, :width].astype(f32)
+
+
+def norm_stats(value):
+    mean = jnp.mean(value, axis=-1, keepdims=True)
+    centred = value - mean
+    variance = jnp.mean(centred * centred, axis=-1, keepdims=True)
+    scale = lax.rsqrt(variance + NORM_EPS)
+    return centred * scale, scale
+
+
+def lane_masks():
+    lane = lax.broadcasted_iota(jnp.int32, (1, 2 * HEAD), 1)
+    return lane < HEAD, lane >= HEAD
+
+
+def swap_halves(value):
+    return pltpu.roll(value, HEAD, 1)
+
+
+def attn_forward_kernel(layer_no, n_heads, length_ref, blocks_ref, *refs):
+    if layer_no == 0:
+        x_ref, refs = refs[0], refs[1:]
+    else:
+        hidden_ref, part_a, part_b, refs = refs[0], refs[1], refs[2], refs[3:]
+        small_prev, refs = refs[:3], refs[3:]
+    small_c, wqkv_c, wout_c, fm_c, refs = refs[:3], refs[3:6], refs[6:9], refs[9:12], refs[12:]
+    if layer_no == 1:
+        x_ref, refs = refs[0], refs[1:]
+    (branch_ref, qkv_out, normed_out, probs_out, qf_out, kf_out, mt_out, mixed_out) = refs[:8]
+    (small, wqkv, wout, fm, qkv, normed, probs, qfeat, kfeat, mt, mixed, fcat, perf, qmask,
+     in_sem, out_sem) = refs[8:24]
+    seq, width = normed.shape
+    n_chunks = seq // ROWS
+    pairs = n_heads // 2
+    feat = fm.shape[2]
+    source = pick_source(layer_no)
+    if layer_no == 1:
+        small_before = refs[24]
+        before = pick_source(0)
+        start_pick(before, small_prev, small_before, in_sem.at[4])
+    start_pick(source, small_c, small, in_sem.at[0])
+    start_pick(source, wqkv_c, wqkv, in_sem.at[1])
+    start_pick(source, fm_c, fm, in_sem.at[2])
+    start_pick(source, wout_c, wout, in_sem.at[3])
+    wait_pick(small_c, small, in_sem.at[0])
+    if layer_no == 1:
+        wait_pick(small_prev, small_before, in_sem.at[4])
+    wait_pick(wqkv_c, wqkv, in_sem.at[1])
+    length = length_ref[0]
+    gain = 1.0 + small_row(small, 4, width)
+    shift = small_row(small, 5, width)
+
+    @pl.loop(0, n_chunks)
+    def _(chunk):
+        rows = pl.ds(pl.multiple_of(chunk * ROWS, ROWS), ROWS)
+        if layer_no == 0:
+            x = x_ref[rows, :].astype(f32)
+        else:
+            total = part_a[rows, :].astype(f32) + part_b[rows, :].astype(f32)
+            x_low = (hidden_ref[rows, :] + total + small_row(small_before, 9, width)).astype(bf)
+            x_ref[rows, :] = x_low
+            x = x_low.astype(f32)
+        zhat, _ = norm_stats(x)
+        low = (zhat * gain + shift).astype(bf)
+        normed[rows, :] = low
+        for part in range(3):
+            cols = n_heads * HEAD
+            out = jnp.dot(low, wqkv[part], preferred_element_type=f32)
+            qkv[part, rows, :] = (out + small_row(small, part, cols)).astype(bf)
+
+    copies = [
+        pltpu.make_async_copy(qkv, qkv_out, out_sem.at[0]),
+        pltpu.make_async_copy(normed, normed_out, out_sem.at[1]),
+    ]
+    for copy in copies:
+        copy.start()
+    wait_pick(fm_c, fm, in_sem.at[2])
+    in_first, in_second = lane_masks()
+    masks = (in_first, in_second)
+    for pair in range(pairs):
+        cols = slice(pair * 2 * HEAD, (pair + 1) * 2 * HEAD)
+        zero = jnp.zeros((HEAD, feat), bf)
+        for a in range(2):
+            scaled = fm[2 * pair + a] * (F_SCALE * LOG2E)
+            high = scaled.astype(bf)
+            rest = (scaled - high.astype(f32)).astype(bf)
+            for part, piece in enumerate((high, rest)):
+                row = part * 2 * HEAD + a * HEAD
+                fcat[row : row + HEAD, a * feat : (a + 1) * feat] = piece
+                fcat[row : row + HEAD, (1 - a) * feat : (2 - a) * feat] = zero
+
+        def features(vectors):
+            proj = jnp.dot(
+                jnp.concatenate([vectors, vectors], axis=1), fcat[...], preferred_element_type=f32
+            )
+            value = vectors.astype(f32)
+            square = value * value * (0.5 * F_SCALE * F_SCALE * LOG2E)
+            return [
+                jnp.exp2(
+                    proj[:, a * feat : (a + 1) * feat]
+                    - jnp.sum(jnp.where(masks[a], square, 0.0), axis=-1, keepdims=True)
+                )
+                for a in range(2)
+            ]
+
+        @pl.loop(0, n_chunks)
+        def _(chunk):
+            base = pl.multiple_of(chunk * ROWS, ROWS)
+            rows = pl.ds(base, ROWS)
+            live = lax.broadcasted_iota(jnp.int32, (ROWS, 1), 0) + base < length
+            found = features(qkv[1, rows, cols])
+            for a in range(2):
+                kfeat[pair, rows, a * feat : (a + 1) * feat] = jnp.where(live, found[a], 0.0).astype(bf)
+
+        values = qkv[2, :, cols].astype(f32)
+        for a in range(2):
+            extended = jnp.where(masks[a], values, 1.0).astype(bf)
+            moment = contract(extended, kfeat[pair, :, a * feat : (a + 1) * feat], 0, 0)
+            mt[2 * pair + a] = moment.astype(bf)
+
+        @pl.loop(0, n_chunks)
+        def _(chunk):
+            rows = pl.ds(pl.multiple_of(chunk * ROWS, ROWS), ROWS)
+            query = qkv[0, rows, cols]
+            found = features(query)
+            out = None
+            for a in range(2):
+                low = found[a].astype(bf)
+                qfeat[pair, rows, a * feat : (a + 1) * feat] = low
+                numer = contract(low, mt[2 * pair + a], 1, 1)
+                value = numer / swap_halves(numer)
+                out = value if a == 0 else jnp.where(in_first, out, value)
+                scaled = query.astype(f32) * (HEAD ** -0.5)
+                qmask[a, rows, :] = jnp.where(masks[a], scaled, 0.0).astype(bf)
+            perf[rows, :] = out
+
+        lane = lax.broadcasted_iota(jnp.int32, (1, 4 * BLOCK), 1)
+        within = lax.rem(lane, BLOCK)
+
+        @pl.loop(0, seq // BLOCK, unroll=2)
+        def _(block):
+            rows = pl.ds(pl.multiple_of(block * BLOCK, BLOCK), BLOCK)
+            out = None
+            for a in range(2):
+                head = 2 * pair + a
+                at = (head * (seq // BLOCK) + block) * 3
+                starts = [pl.multiple_of(blocks_ref[at + i] * BLOCK, BLOCK) for i in range(3)]
+                keys = jnp.concatenate(
+                    [qkv[1, 0:BLOCK, cols]] + [qkv[1, pl.ds(b, BLOCK), cols] for b in starts], axis=0
+                )
+                values = jnp.concatenate(
+                    [qkv[2, 0:BLOCK, cols]] + [qkv[2, pl.ds(b, BLOCK), cols] for b in starts], axis=0
+                )
+                position = within + jnp.where(
+                    lane < BLOCK,
+                    0,
+                    jnp.where(
+                        lane < 2 * BLOCK,
+                        starts[0],
+                        jnp.where(lane < 3 * BLOCK, starts[1], starts[2]),
+                    ),
+                )
+                scores = contract(qmask[a, rows, :], keys, 1, 1)
+                scores = jnp.where(position < length, scores, -1e30)
+                top = jnp.max(scores, axis=-1, keepdims=True)
+                raw = jnp.exp(scores - top)
+                low = (raw * (1.0 / jnp.sum(raw, axis=-1, keepdims=True))).astype(bf)
+                probs[head, rows, :] = low
+                value = jnp.dot(low, values, preferred_element_type=f32)
+                out = value if a == 0 else jnp.where(in_first, out, value)
+            mixed[rows, cols] = (out + perf[rows, :]).astype(bf)
+
+        more = [
+            pltpu.make_async_copy(probs.at[2 * pair : 2 * pair + 2], probs_out.at[2 * pair : 2 * pair + 2], out_sem.at[2 + 4 * pair]),
+            pltpu.make_async_copy(qfeat.at[pair], qf_out.at[pair], out_sem.at[3 + 4 * pair]),
+            pltpu.make_async_copy(kfeat.at[pair], kf_out.at[pair], out_sem.at[4 + 4 * pair]),
+            pltpu.make_async_copy(mt.at[2 * pair : 2 * pair + 2], mt_out.at[2 * pair : 2 * pair + 2], out_sem.at[5 + 4 * pair]),
+        ]
+        for copy in more:
+            copy.start()
+        copies += more
+    wait_pick(wout_c, wout, in_sem.at[3])
+
+    @pl.loop(0, n_chunks)
+    def _(chunk):
+        rows = pl.ds(pl.multiple_of(chunk * ROWS, ROWS), ROWS)
+        low = mixed[rows, :]
+        mixed_out[rows, :] = low
+        branch_ref[rows, :] = jnp.dot(low, wout[...], preferred_element_type=f32).astype(bf)
+
+    for copy in copies:
+        copy.wait()
+
+
+def attn_forward(layer_no, length, blocks, x_parts, weights, small_before):
+    small_c, wqkv_c, wout_c, fm_c = weights
+    _, width, part_width = wqkv_c[0].shape
+    n_heads, _, feat = fm_c[0].shape
+    seq = x_parts[0].shape[0]
+    pairs = n_heads // 2
+    shape = jax.ShapeDtypeStruct
+    outs = [
+        shape((seq, width), bf),
+        shape((3, seq, part_width), bf),
+        shape((seq, width), bf),
+        shape((n_heads, seq, 4 * BLOCK), bf),
+        shape((pairs, seq, 2 * feat), bf),
+        shape((pairs, seq, 2 * feat), bf),
+        shape((n_heads, 2 * HEAD, feat), bf),
+        shape((seq, part_width), bf),
+    ]
+    out_specs = [WHOLE, ANY, ANY, ANY, ANY, ANY, ANY, WHOLE]
+    scratch = [
+        pltpu.VMEM(small_c[0].shape, bf),
+        pltpu.VMEM(wqkv_c[0].shape, bf),
+        pltpu.VMEM(wout_c[0].shape, bf),
+        pltpu.VMEM(fm_c[0].shape, f32),
+        pltpu.VMEM((3, seq, part_width), bf),
+        pltpu.VMEM((seq, width), bf),
+        pltpu.VMEM((n_heads, seq, 4 * BLOCK), bf),
+        pltpu.VMEM((pairs, seq, 2 * feat), bf),
+        pltpu.VMEM((pairs, seq, 2 * feat), bf),
+        pltpu.VMEM((n_heads, 2 * HEAD, feat), bf),
+        pltpu.VMEM((seq, part_width), bf),
+        pltpu.VMEM((4 * HEAD, 2 * feat), bf),
+        pltpu.VMEM((seq, 2 * HEAD), f32),
+        pltpu.VMEM((2, seq, 2 * HEAD), bf),
+        pltpu.SemaphoreType.DMA((5,)),
+        pltpu.SemaphoreType.DMA((2 + 4 * pairs,)),
+    ]
+    operands = list(x_parts)
+    specs = [WHOLE] * len(x_parts)
+    if layer_no == 1:
+        operands += list(small_before)
+        specs += [ANY] * 3
+        outs = [shape((seq, width), bf)] + outs
+        out_specs = [WHOLE] + out_specs
+        scratch.append(pltpu.VMEM(small_c[0].shape, bf))
+    for group in weights:
+        operands += list(group)
+        specs += [ANY] * 3
+    return pl.pallas_call(
+        functools.partial(attn_forward_kernel, layer_no, n_heads),
+        out_shape=outs,
+        in_specs=[SCALARS, SCALARS] + specs,
+        out_specs=out_specs,
+        scratch_shapes=scratch,
+        compiler_params=pltpu.CompilerParams(vmem_limit_bytes=VMEM_BYTES),
+        cost_estimate=pl.CostEstimate(
+            flops=4 * 10**9, bytes_accessed=16 * 2**20, transcendentals=3 * 2**20
+        ),
+        name=f"attn_forward_{layer_no}",
+    )(length, blocks, *operands)
+
+
+def gelu_parts(value):
+    size = jnp.abs(value) * (0.5 ** 0.5)
+    inverse = 1.0 / (1.0 + 0.3275911 * size)
+    poly = inverse * (
+        0.254829592
+        + inverse
+        * (-0.284496736 + inverse * (1.421413741 + inverse * (-1.453152027 + inverse * 1.061405429)))
+    )
+    bell = jnp.exp(-0.5 * value * value)
+    tail = 0.5 * poly * bell
+    below = jnp.where(value >= 0.0, 1.0 - tail, tail)
+    return value * below, below + value * bell * (0.5 / 3.141592653589793) ** 0.5
+
+
+def ffn_forward_kernel(layer_no, n_in, *refs):
+    x_ref, part_a, part_b = refs[:3]
+    small_c, wup_c, wdown_c = refs[3:6], refs[6:9], refs[9:12]
+    out_ref, hidden_ref, normed_ref, active_ref, slope_ref = refs[12:17]
+    small, wup, wdown, sems = refs[17:]
+
+    @pl.when(pl.program_id(0) == 0)
+    def _():
+        source = pick_source(layer_no)
+        start_pick(source, small_c, small, sems.at[0])
+        start_pick(source, wup_c, wup, sems.at[1])
+        start_pick(source, wdown_c, wdown, sems.at[2])
+        wait_pick(small_c, small, sems.at[0])
+        wait_pick(wup_c, wup, sems.at[1])
+        wait_pick(wdown_c, wdown, sems.at[2])
+
+    width = x_ref.shape[1]
+    units = wup.shape[1]
+    branch = part_a[...].astype(f32) + part_b[...].astype(f32)
+    hidden = x_ref[...].astype(f32) + branch + small_row(small, 8, width)
+    hidden_ref[...] = hidden
+    zhat, _ = norm_stats(hidden)
+    low = (zhat * (1.0 + small_row(small, 6, width)) + small_row(small, 7, width)).astype(bf)
+    normed_ref[...] = low
+    total = None
+    step = 256
+    for at in range(0, units, step):
+        upper = jnp.dot(low, wup[:, at : at + step], preferred_element_type=f32)
+        active, slope = gelu_parts(upper + small[3:4, at : at + step].astype(f32))
+        active = active.astype(bf)
+        active_ref[:, at : at + step] = active
+        slope_ref[:, at : at + step] = slope.astype(bf)
+        term = jnp.dot(active, wdown[at : at + step, :], preferred_element_type=f32)
+        total = term if total is None else total + term
+    out_ref[...] = total.astype(bf)
+
+
+def ffn_forward(layer_no, x, part_a, part_b, weights):
+    small_c, wup_c, wdown_c = weights
+    seq, width = x.shape
+    units = wup_c[0].shape[1]
+    shape = jax.ShapeDtypeStruct
+    rows = lambda cols: pl.BlockSpec((ROWS, cols), lambda i: (i, 0))
+    return pl.pallas_call(
+        functools.partial(ffn_forward_kernel, layer_no, 3),
+        grid=(seq // ROWS,),
+        out_shape=[
+            shape((seq, width), bf),
+            shape((seq, width), f32),
+            shape((seq, width), bf),
+            shape((seq, units), bf),
+            shape((seq, units), bf),
+        ],
+        in_specs=[rows(width)] * 3 + [ANY] * 9,
+        out_specs=[rows(width), rows(width), rows(width), rows(units), rows(units)],
+        scratch_shapes=[
+            pltpu.VMEM(small_c[0].shape, bf),
+            pltpu.VMEM(wup_c[0].shape, bf),
+            pltpu.VMEM(wdown_c[0].shape, bf),
+            pltpu.SemaphoreType.DMA((3,)),
+        ],
+        compiler_params=pltpu.CompilerParams(vmem_limit_bytes=VMEM_BYTES),
+        cost_estimate=pl.CostEstimate(
+            flops=4 * seq * width * units, bytes_accessed=14 * 2**20, transcendentals=seq * units
+        ),
+        name=f"ffn_forward_{layer_no}",
+    )(x, part_a, part_b, *small_c, *wup_c, *wdown_c)
+
+
+def ffn_backward_kernel(layer_no, grad_ref, slope_ref, *refs):
+    wup_c, wdown_c = refs[:3], refs[3:6]
+    out_ref, gupper_ref, bias_ref = refs[6:9]
+    wup, wdown, sems = refs[9:]
+
+    @pl.when(pl.program_id(0) == 0)
+    def _():
+        source = pick_source(layer_no)
+        start_pick(source, wdown_c, wdown, sems.at[0])
+        start_pick(source, wup_c, wup, sems.at[1])
+        bias_ref[...] = jnp.zeros_like(bias_ref)
+        wait_pick(wdown_c, wdown, sems.at[0])
+        wait_pick(wup_c, wup, sems.at[1])
+
+    units = wup.shape[1]
+    grad = grad_ref[...]
+    total = None
+    step = 256
+    for at in range(0, units, step):
+        gactive = contract(grad, wdown[at : at + step, :], 1, 1)
+        gupper = (gactive * slope_ref[:, at : at + step].astype(f32)).astype(bf)
+        gupper_ref[:, at : at + step] = gupper
+        bias_ref[:, at : at + step] += fold_rows(gupper.astype(f32))
+        term = contract(gupper, wup[:, at : at + step], 1, 1)
+        total = term if total is None else total + term
+    out_ref[...] = total.astype(bf)
+
+
+def fold_rows(value):
+    rows, cols = value.shape
+    return jnp.sum(value.reshape(rows // 8, 8, cols), axis=0)
+
+
+def ffn_backward(layer_no, grad, slope, weights):
+    wup_c, wdown_c = weights
+    seq, width = grad.shape
+    units = wup_c[0].shape[1]
+    shape = jax.ShapeDtypeStruct
+    rows = lambda cols: pl.BlockSpec((ROWS, cols), lambda i: (i, 0))
+    return pl.pallas_call(
+        functools.partial(ffn_backward_kernel, layer_no),
+        grid=(seq // ROWS,),
+        out_shape=[shape((seq, width), bf), shape((seq, units), bf), shape((8, units), f32)],
+        in_specs=[rows(width), rows(units)] + [ANY] * 6,
+        out_specs=[rows(width), rows(units), pl.BlockSpec((8, units), lambda i: (0, 0))],
+        scratch_shapes=[
+            pltpu.VMEM(wup_c[0].shape, bf),
+            pltpu.VMEM(wdown_c[0].shape, bf),
+            pltpu.SemaphoreType.DMA((2,)),
+        ],
+        compiler_params=pltpu.CompilerParams(vmem_limit_bytes=VMEM_BYTES),
+        cost_estimate=pl.CostEstimate(
+            flops=4 * seq * width * units, bytes_accessed=8 * 2**20, transcendentals=0
+        ),
+        name=f"ffn_backward_{layer_no}",
+    )(grad, slope, *wup_c, *wdown_c)
+
+
+def attn_backward_kernel(layer_no, n_heads, blocks_ref, *refs):
+    gy_ref, part_a, part_b, hidden_ref = refs[:4]
+    qkv_in, probs_in, qf_in, kf_in, mt_in = refs[4:9]
+    small_c, wqkv_c, wout_c, fm_c, refs = refs[9:12], refs[12:15], refs[15:18], refs[18:21], refs[21:]
+    out_ref, ghidden_ref, gbranch_ref, dqkv_ref, vec_ref, bias_ref, refs = *refs[:6], refs[6:]
+    (small, wqkv, wout, fm, qkv, probs, qfeat, kfeat, mt, gmix, gmask, qmask, gext, gt, fback,
+     dq, dk, dv, sem) = refs
+    seq, width = gy_ref.shape
+    n_chunks = seq // ROWS
+    pairs = n_heads // 2
+    feat = fm.shape[2]
+    source = pick_source(layer_no)
+    start_pick(source, small_c, small, sem.at[0])
+    start_pick(source, wout_c, wout, sem.at[1])
+    loads = [
+        pltpu.make_async_copy(qkv_in, qkv, sem.at[2]),
+        pltpu.make_async_copy(mt_in, mt, sem.at[3]),
+        pltpu.make_async_copy(qf_in, qfeat, sem.at[4]),
+        pltpu.make_async_copy(kf_in, kfeat, sem.at[5]),
+        pltpu.make_async_copy(probs_in, probs, sem.at[6]),
+    ]
+    for load in loads:
+        load.start()
+    start_pick(source, fm_c, fm, sem.at[7])
+    start_pick(source, wqkv_c, wqkv, sem.at[8])
+    vec_ref[...] = jnp.zeros_like(vec_ref)
+    bias_ref[...] = jnp.zeros_like(bias_ref)
+    wait_pick(small_c, small, sem.at[0])
+    wait_pick(wout_c, wout, sem.at[1])
+    gain = 1.0 + small_row(small, 6, width)
+    in_first, in_second = lane_masks()
+    masks = (in_first, in_second)
+
+    @pl.loop(0, n_chunks)
+    def _(chunk):
+        rows = pl.ds(pl.multiple_of(chunk * ROWS, ROWS), ROWS)
+        gnormed = part_a[rows, :].astype(f32) + part_b[rows, :].astype(f32)
+        zhat, scale = norm_stats(hidden_ref[rows, :])
+        scaled = gnormed * gain
+        gy = gy_ref[rows, :].astype(f32)
+        mean_one = jnp.mean(scaled, axis=-1, keepdims=True)
+        mean_two = jnp.mean(scaled * zhat, axis=-1, keepdims=True)
+        ghidden = gy + (scaled - mean_one - zhat * mean_two) * scale
+        ghidden_ref[rows, :] = ghidden
+        low = ghidden.astype(bf)
+        gbranch_ref[rows, :] = low
+        vec_ref[0] += fold_rows(gnormed * zhat)
+        vec_ref[1] += fold_rows(gnormed)
+        vec_ref[2] += fold_rows(low.astype(f32))
+        vec_ref[3] += fold_rows(gy)
+        gmix_low = contract(low, wout[...], 1, 1).astype(bf)
+        gmix[rows, :] = gmix_low
+
+    for load in loads[:4]:
+        load.wait()
+    wait_pick(fm_c, fm, sem.at[7])
+    for pair in range(pairs):
+        cols = slice(pair * 2 * HEAD, (pair + 1) * 2 * HEAD)
+        for a in range(2):
+            plain = fm[2 * pair + a] * F_SCALE
+            high = plain.astype(bf).astype(f32)
+            ones = jnp.ones((HEAD, feat), f32)
+            none = jnp.zeros((HEAD, feat), f32)
+            stack = [high, ones] if a == 0 else [ones, high]
+            stack += [plain - high, none] if a == 0 else [none, plain - high]
+            fback[a] = jnp.concatenate(stack, axis=0).astype(bf)
+
+        def feature_back(a, gfeat, feats, vectors):
+            gexpo = (gfeat * feats.astype(f32)).astype(bf)
+            both = contract(gexpo, fback[a], 1, 1)
+            both = both[:, : 2 * HEAD] + both[:, 2 * HEAD :]
+            return both - (F_SCALE * F_SCALE) * swap_halves(both) * vectors
+
+        @pl.loop(0, n_chunks)
+        def _(chunk):
+            rows = pl.ds(pl.multiple_of(chunk * ROWS, ROWS), ROWS)
+            grad = gmix[rows, cols].astype(f32)
+            query = qkv[0, rows, cols].astype(f32)
+            out = None
+            for a in range(2):
+                gmask[a, rows, :] = jnp.where(masks[a], grad, 0.0).astype(bf)
+                qmask[a, rows, :] = jnp.where(masks[a], query * (HEAD ** -0.5), 0.0).astype(bf)
+                feats = qfeat[pair, rows, a * feat : (a + 1) * feat]
+                moment = mt[2 * pair + a]
+                numer = contract(feats, moment, 1, 1)
+                inverse = 1.0 / swap_halves(numer)
+                gnumer = grad * inverse
+                other = swap_halves(gnumer * numer * inverse)
+                both = jnp.where(masks[a], gnumer, -other).astype(bf)
+                gext[a, rows, :] = both
+                gfeat = jnp.dot(both, moment, preferred_element_type=f32)
+                value = feature_back(a, gfeat, feats, query)
+                out = value if a == 0 else jnp.where(in_first, out, value)
+            dq[rows, :] = out
+
+        for a in range(2):
+            gt[a] = contract(gext[a], qfeat[pair, :, a * feat : (a + 1) * feat], 0, 0).astype(bf)
+
+        @pl.loop(0, n_chunks)
+        def _(chunk):
+            rows = pl.ds(pl.multiple_of(chunk * ROWS, ROWS), ROWS)
+            key = qkv[1, rows, cols].astype(f32)
+            value_f = qkv[2, rows, cols].astype(f32)
+            dk_out, dv_out = None, None
+            for a in range(2):
+                extended = jnp.where(masks[a], value_f, 1.0).astype(bf)
+                feats = kfeat[pair, rows, a * feat : (a + 1) * feat]
+                gfeat = jnp.dot(extended, gt[a], preferred_element_type=f32)
+                dk_one = feature_back(a, gfeat, feats, key)
+                dv_one = contract(feats, gt[a], 1, 1)
+                dk_out = dk_one if a == 0 else jnp.where(in_first, dk_out, dk_one)
+                dv_out = dv_one if a == 0 else jnp.where(in_first, dv_out, dv_one)
+            dk[rows, :] = dk_out
+            dv[rows, :] = dv_out
+
+        if pair == 0:
+            loads[4].wait()
+
+        @pl.loop(0, seq // BLOCK, unroll=2)
+        def _(block):
+            rows = pl.ds(pl.multiple_of(block * BLOCK, BLOCK), BLOCK)
+            out = None
+            for a in range(2):
+                head = 2 * pair + a
+                at = (head * (seq // BLOCK) + block) * 3
+                starts = [pl.multiple_of(blocks_ref[at + i] * BLOCK, BLOCK) for i in range(3)]
+                keys = jnp.concatenate(
+                    [qkv[1, 0:BLOCK, cols]] + [qkv[1, pl.ds(b, BLOCK), cols] for b in starts], axis=0
+                )
+                values = jnp.concatenate(
+                    [qkv[2, 0:BLOCK, cols]] + [qkv[2, pl.ds(b, BLOCK), cols] for b in starts], axis=0
+                )
+                grad = gmask[a, rows, :]
+                weights = probs[head, rows, :]
+                weights_f = weights.astype(f32)
+                gweights = contract(grad, values, 1, 1)
+                inner = jnp.sum(weights_f * gweights, axis=-1, keepdims=True)
+                gscores = (weights_f * (gweights - inner)).astype(bf)
+                value = jnp.dot(gscores, keys, preferred_element_type=f32) * (HEAD ** -0.5)
+                out = value if a == 0 else jnp.where(in_first, out, value)
+                dkeys = contract(gscores, qmask[a, rows, :], 0, 0)
+                dvalues = contract(weights, grad, 0, 0)
+                for slot, start in enumerate([0] + starts):
+                    here = slice(slot * BLOCK, (slot + 1) * BLOCK)
+                    dk[pl.ds(start, BLOCK), :] += dkeys[here, :]
+                    dv[pl.ds(start, BLOCK), :] += dvalues[here, :]
+            dq[rows, :] += out
+
+        @pl.loop(0, n_chunks)
+        def _(chunk):
+            rows = pl.ds(pl.multiple_of(chunk * ROWS, ROWS), ROWS)
+            for part, total in enumerate((dq, dk, dv)):
+                low = total[rows, :].astype(bf)
+                dqkv_ref[part, rows, cols] = low
+                bias_ref[part, :, cols] += fold_rows(low.astype(f32))
+
+    wait_pick(wqkv_c, wqkv, sem.at[8])
+
+    @pl.loop(0, n_chunks)
+    def _(chunk):
+        rows = pl.ds(pl.multiple_of(chunk * ROWS, ROWS), ROWS)
+        total = None
+        for part in range(3):
+            term = contract(dqkv_ref[part, rows, :], wqkv[part], 1, 1)
+            total = term if total is None else total + term
+        out_ref[rows, :] = total.astype(bf)
+
+
+def attn_backward(layer_no, blocks, gy, part_a, part_b, hidden, kept, weights):
+    small_c, wqkv_c, wout_c, fm_c = weights
+    seq, width = gy.shape
+    _, _, part_width = wqkv_c[0].shape
+    n_heads, _, feat = fm_c[0].shape
+    pairs = n_heads // 2
+    shape = jax.ShapeDtypeStruct
+    operands = [gy, part_a, part_b, hidden, *kept]
+    for group in weights:
+        operands += list(group)
+    return pl.pallas_call(
+        functools.partial(attn_backward_kernel, layer_no, n_heads),
+        out_shape=[
+            shape((seq, width), bf),
+            shape((seq, width), f32),
+            shape((seq, width), bf),
+            shape((3, seq, part_width), bf),
+            shape((4, 8, width), f32),
+            shape((3, 8, part_width), f32),
+        ],
+        in_specs=[SCALARS] + [WHOLE] * 4 + [ANY] * 17,
+        out_specs=[WHOLE] * 6,
+        scratch_shapes=[
+            pltpu.VMEM(small_c[0].shape, bf),
+            pltpu.VMEM(wqkv_c[0].shape, bf),
+            pltpu.VMEM(wout_c[0].shape, bf),
+            pltpu.VMEM(fm_c[0].shape, f32),
+            pltpu.VMEM((3, seq, part_width), bf),
+            pltpu.VMEM((n_heads, seq, 4 * BLOCK), bf),
+            pltpu.VMEM((pairs, seq, 2 * feat), bf),
+            pltpu.VMEM((pairs, seq, 2 * feat), bf),
+            pltpu.VMEM((n_heads, 2 * HEAD, feat), bf),
+            pltpu.VMEM((seq, part_width), bf),
+            pltpu.VMEM((2, seq, 2 * HEAD), bf),
+            pltpu.VMEM((2, seq, 2 * HEAD), bf),
+            pltpu.VMEM((2, seq, 2 * HEAD), bf),
+            pltpu.VMEM((2, 2 * HEAD, feat), bf),
+            pltpu.VMEM((2, 4 * HEAD, feat), bf),
+            pltpu.VMEM((seq, 2 * HEAD), f32),
+            pltpu.VMEM((seq, 2 * HEAD), f32),
+            pltpu.VMEM((seq, 2 * HEAD), f32),
+            pltpu.SemaphoreType.DMA((9,)),
+        ],
+        compiler_params=pltpu.CompilerParams(vmem_limit_bytes=VMEM_BYTES),
+        cost_estimate=pl.CostEstimate(
+            flops=8 * 10**9, bytes_accessed=20 * 2**20, transcendentals=2**20
+        ),
+        name=f"attn_backward_{layer_no}",
+    )(blocks, *operands)
+
+
+def norm_backward_kernel(layer_no, x_ref, part_a, part_b, ghidden_ref, *refs):
+    small_c = refs[:3]
+    out_ref, low_ref, vec_ref, small, sems = refs[3:]
+
+    @pl.when(pl.program_id(0) == 0)
+    def _():
+        start_pick(pick_source(layer_no), small_c, small, sems.at[0])
+        vec_ref[...] = jnp.zeros_like(vec_ref)
+        wait_pick(small_c, small, sems.at[0])
+
+    width = x_ref.shape[1]
+    gnormed = part_a[...].astype(f32) + part_b[...].astype(f32)
+    zhat, scale = norm_stats(x_ref[...].astype(f32))
+    scaled = gnormed * (1.0 + small_row(small, 4, width))
+    mean_one = jnp.mean(scaled, axis=-1, keepdims=True)
+    mean_two = jnp.mean(scaled * zhat, axis=-1, keepdims=True)
+    total = ghidden_ref[...] + (scaled - mean_one - zhat * mean_two) * scale
+    out_ref[...] = total
+    low_ref[...] = total.astype(bf)
+    vec_ref[0] += fold_rows(gnormed * zhat)
+    vec_ref[1] += fold_rows(gnormed)
+
+
+def norm_backward(layer_no, x, part_a, part_b, ghidden, small_c):
+    seq, width = x.shape
+    shape = jax.ShapeDtypeStruct
+    rows = pl.BlockSpec((ROWS, width), lambda i: (i, 0))
+    return pl.pallas_call(
+        functools.partial(norm_backward_kernel, layer_no),
+        grid=(seq // ROWS,),
+        out_shape=[shape((seq, width), f32), shape((seq, width), bf), shape((2, 8, width), f32)],
+        in_specs=[rows] * 4 + [ANY] * 3,
+        out_specs=[rows, rows, pl.BlockSpec((2, 8, width), lambda i: (0, 0, 0))],
+        scratch_shapes=[pltpu.VMEM(small_c[0].shape, bf), pltpu.SemaphoreType.DMA((1,))],
+        compiler_params=pltpu.CompilerParams(vmem_limit_bytes=VMEM_BYTES),
+        cost_estimate=pl.CostEstimate(
+            flops=20 * seq * width, bytes_accessed=8 * 2**20, transcendentals=0
+        ),
+        name=f"norm_backward_{layer_no}",
+    )(x, part_a, part_b, ghidden, *small_c)
+
+
+def weight_grad_kernel(split, n_first, left_a, left_b, right_a, right_b, out_ref, turned):
+    step = pl.program_id(0)
+    _, n_rows, shard, cols = out_ref.shape
+
+    @pl.when(step == 0)
+    def _():
+        turned[...] = left_a[...].T
+
+    @pl.when(step == n_first)
+    def _():
+        turned[...] = left_b[...].T
+
+    def emit(right):
+        result = jnp.dot(turned[...], right, preferred_element_type=f32).astype(bf)
+        for number in range(split * n_rows):
+            out_ref[number % split, number // split] = result[number * shard : (number + 1) * shard]
+
+    @pl.when(step < n_first)
+    def _():
+        emit(right_a[...])
+
+    @pl.when(step >= n_first)
+    def _():
+        emit(right_b[...])
+
+
+def weight_grads(name, dp_count, left_a, right_a, left_b, right_b):
+    seq, width = left_a.shape
+    step = 256
+    if right_a.ndim == 3:
+        n_first = right_a.shape[0]
+        step = right_a.shape[2]
+        spec_a = pl.BlockSpec((None, seq, step), lambda i: (jnp.minimum(i, n_first - 1), 0, 0))
+    else:
+        n_first = right_a.shape[1] // step
+        spec_a = pl.BlockSpec((seq, step), lambda i: (0, jnp.minimum(i, n_first - 1)))
+    n_second = right_b.shape[1] // step
+    spec_b = pl.BlockSpec((seq, step), lambda i: (0, jnp.maximum(i - n_first, 0)))
+    whole = pl.BlockSpec((seq, width), lambda i: (0, 0))
+    n_steps = n_first + n_second
+    shape = (2, dp_count // 2, width // dp_count, step * n_steps)
+    return pl.pallas_call(
+        functools.partial(weight_grad_kernel, 2, n_first),
+        grid=(n_steps,),
+        out_shape=jax.ShapeDtypeStruct(shape, bf),
+        in_specs=[whole, whole, spec_a, spec_b],
+        out_specs=pl.BlockSpec(shape[:3] + (step,), lambda i: (0, 0, 0, i)),
+        scratch_shapes=[pltpu.VMEM((width, seq), bf)],
+        compiler_params=pltpu.CompilerParams(vmem_limit_bytes=VMEM_BYTES),
+        cost_estimate=pl.CostEstimate(
+            flops=2 * seq * width * step * n_steps, bytes_accessed=8 * 2**20, transcendentals=0
+        ),
+        name=name,
+    )(left_a, left_b, right_a, right_b)
+
+
+ALL_AXES = ("section", "tensor", "dp")
+
+
+def send(value, sizes, target):
+    n_section, n_tensor, n_dp = sizes
+    pairs = []
+    for s in range(n_section):
+        for t in range(n_tensor):
+            for d in range(n_dp):
+                goal = target(s, t, d // 2, d % 2)
+                if goal is not None:
+                    gs, gt, gz, gc = goal
+                    number = (s * n_tensor + t) * n_dp + d
+                    pairs.append((number, (gs * n_tensor + gt) * n_dp + 2 * gz + gc))
+    return lax.ppermute(value, ALL_AXES, pairs)
+
+
+def other_core(value, sizes):
+    return send(value, sizes, lambda s, t, z, c: (s, t, z, 1 - c))
+
+
+def chip_shards(
+    sizes,
+    inputs,
+    cotangent,
+    lengths,
+    blocks,
+    feature_map,
+    w_qkv,
+    b_qkv,
+    w_out,
+    w_up,
+    b_up,
+    w_down,
+    vector_params,
+):
+    n_dp = sizes[2]
+    n_z = n_dp // 2
+    section_no = lax.axis_index("section")
+    tensor_no = lax.axis_index("tensor")
+    dp_no = lax.axis_index("dp")
+    z_no, core = dp_no // 2, dp_no % 2
+    same = core == tensor_no
+    is_first = section_no == 0
+    width = inputs.shape[2]
+    half = inputs.shape[1]
+    n_heads, n_blocks, n_listed = blocks.shape[1:]
+    units = w_up.shape[2]
+    part_width = w_qkv.shape[3]
+
+    def to_sequence(array):
+        own = array[section_no]
+        first = send(
+            own,
+            sizes,
+            lambda s, t, z, c: (s, t, z, 1 - c) if c == t else (s, 1 - t, z, c),
+        )
+        second = send(first, sizes, lambda s, t, z, c: (s, t, z, 1 - c) if c == t else None)
+        near = jnp.where(same, own, first)
+        far = jnp.where(same, first, second)
+        swap = tensor_no == 1
+        return jnp.concatenate(
+            [jnp.where(swap, far, near), jnp.where(swap, near, far)], axis=0
+        )
+
+    x_first = to_sequence(inputs)
+
+    def lane_row(array, count):
+        flat = array.reshape(count, -1)
+        return jnp.pad(flat, ((0, 0), (0, units - flat.shape[1])))
+
+    small = jnp.concatenate(
+        [
+            lane_row(b_qkv, 3),
+            lane_row(b_up, 1),
+            lane_row(vector_params, 6),
+            lane_row(blocks.astype(bf), 1),
+            jnp.zeros((5, units), bf),
+        ],
+        axis=0,
+    )
+
+    def spread(array, by_x):
+        first = send(
+            array,
+            sizes,
+            lambda s, t, z, c: (1 - s, t, z, c) if c == t else (s, 1 - t, z, 1 - c),
+        )
+        if by_x:
+            second = send(first, sizes, lambda s, t, z, c: (s, 1 - t, z, c) if c == t else None)
+        else:
+            second = send(first, sizes, lambda s, t, z, c: None if c == t else (1 - s, t, z, c))
+        return (array, first, second)
+
+    small_c = spread(small, True)
+    wqkv_c = spread(w_qkv[0].transpose(1, 0, 2), True)
+    fm_c = spread(feature_map[0], False)
+    wout_c = spread(w_out[0], False)
+    wup_c = spread(w_up[0], True)
+    wdown_c = spread(w_down[0], False)
+
+    lengths_here = jnp.where(same, lengths, other_core(lengths, sizes))
+    length = lax.dynamic_slice_in_dim(lengths_here[:, 0], section_no, 1)
+
+    def of_layer(layer_no, candidates):
+        mine = section_no == layer_no
+        return jnp.where(
+            mine,
+            jnp.where(same, candidates[0], candidates[1]),
+            jnp.where(same, candidates[1], candidates[2]),
+        )
+
+    def exchange(value):
+        return value, other_core(value, sizes)
+
+    kept = []
+    x_parts = (x_first,)
+    outputs = []
+    for layer_no in range(2):
+        smalls = of_layer(layer_no, small_c)
+        listed = smalls[10, : n_heads * n_blocks * n_listed].astype(jnp.int32)
+        made = attn_forward(
+            layer_no, length, listed, x_parts, (small_c, wqkv_c, wout_c, fm_c), small_c
+        )
+        if layer_no == 0:
+            x = x_first
+        else:
+            x, made = made[0], made[1:]
+            outputs.append(x)
+        branch, qkv, normed, probs, qfeat, kfeat, mt, mixed = made
+        result, hidden, normed_two, active, slope = ffn_forward(
+            layer_no, x, *exchange(branch), (small_c, wup_c, wdown_c)
+        )
+        x_parts = (hidden, *exchange(result))
+        kept.append(
+            (x, normed, mixed, hidden, normed_two, active, slope, listed,
+             (qkv, probs, qfeat, kfeat, mt))
+        )
+
+    grad = to_sequence(cotangent)
+
+    def my_half(array):
+        return lax.dynamic_slice_in_dim(array, core * half, half)
+
+    def deliver(layer_no, rows):
+        own = send(rows, sizes, lambda s, t, z, c: (s, c, z, t) if s == layer_no else None)
+        other = send(rows, sizes, lambda s, t, z, c: None if s == layer_no else (1 - s, c, z, t))
+        return own, other
+
+    hidden, part_a, part_b = x_parts
+    last_bias = of_layer(1, small_c)[9:10, :width].astype(f32)
+    last = my_half(hidden) + (my_half(part_a).astype(f32) + my_half(part_b).astype(f32)) + last_bias
+    out_pairs = [deliver(0, my_half(outputs[0])), deliver(1, last.astype(bf))]
+
+    def gather_sum(layer_no, array):
+        other = send(array, sizes, lambda s, t, z, c: None if c == t else (s, 1 - t, z, c))
+        total = (array.astype(f32) + other.astype(f32)).astype(array.dtype)
+        other = send(
+            total, sizes, lambda s, t, z, c: (1 - s, t, z, c) if c == t and s != layer_no else None
+        )
+        total = (total.astype(f32) + other.astype(f32)).astype(array.dtype)
+        away = lax.dynamic_index_in_dim(total, 1 - core, keepdims=False)
+        stay = lax.dynamic_index_in_dim(total, core, keepdims=False)
+        other = send(
+            away, sizes, lambda s, t, z, c: (s, t, z, 1 - c) if c == t and s == layer_no else None
+        )
+        piece = jnp.where(same, stay, other)
+        total = lax.dynamic_index_in_dim(piece, z_no, keepdims=False).astype(f32)
+        for step in range(1, n_z):
+            shard = lax.dynamic_index_in_dim(piece, (z_no + step) % n_z, keepdims=False)
+            total = total + send(
+                shard,
+                sizes,
+                lambda s, t, z, c: (s, t, (z + step) % n_z, c) if s == layer_no else None,
+            ).astype(f32)
+        return total
+
+    sums = [None, None]
+    grad_pairs = [None, None]
+    for layer_no in (1, 0):
+        x, normed, mixed, hidden, normed_two, active, slope, listed, attn_kept = kept[layer_no]
+        gnormed_two, gupper, bias_up = ffn_backward(layer_no, grad, slope, (wup_c, wdown_c))
+        part_a, part_b = exchange(gnormed_two)
+        wide = weight_grads(f"ffn_grads_{layer_no}", n_dp, normed_two, gupper, grad, active)
+        gnormed, ghidden, gbranch, gproj, vec_two, bias_qkv = attn_backward(
+            layer_no, listed, grad, part_a, part_b, hidden, attn_kept,
+            (small_c, wqkv_c, wout_c, fm_c),
+        )
+        part_a, part_b = exchange(gnormed)
+        narrow = weight_grads(f"attn_grads_{layer_no}", n_dp, normed, gproj, gbranch, mixed)
+        gx, gx_low, vec_one = norm_backward(layer_no, x, part_a, part_b, ghidden, small_c)
+        vectors = jnp.concatenate([jnp.sum(vec_one, axis=1), jnp.sum(vec_two, axis=1)], axis=0)
+        vectors = lax.dynamic_slice_in_dim(vectors, core * (width // 2), width // 2, axis=1)
+
+        def by_shard(array):
+            rows = array.reshape(array.shape[0], n_z, 2, -1)
+            return rows.transpose(2, 1, 0, 3).reshape(2, n_z, -1)
+
+        tiny = jnp.concatenate(
+            [
+                by_shard(vectors),
+                by_shard(jnp.sum(bias_qkv, axis=1)),
+                by_shard(jnp.sum(bias_up, axis=0, keepdims=True)),
+            ],
+            axis=2,
+        )
+        sums[layer_no] = tuple(gather_sum(layer_no, item) for item in (wide, narrow, tiny))
+        grad_pairs[layer_no] = deliver(layer_no, my_half(gx_low))
+        grad = gx_low
+
+    def placed(pairs, dtype):
+        own = jnp.where(is_first, pairs[0][0], pairs[1][0])
+        other = jnp.where(is_first, pairs[0][1], pairs[1][1])
+        return jnp.stack(
+            [jnp.where(is_first, own, other), jnp.where(is_first, other, own)]
+        )[None].astype(dtype)
+
+    section_outputs = placed(out_pairs, bf)
+    input_grads = placed(grad_pairs, f32)
+    wide, narrow, tiny = (jnp.where(is_first, a, b) for a, b in zip(*sums))
+    shard = width // n_dp
+    grad_up, grad_down = wide[:, :units], wide[:, units:].T
+    grad_qkv = narrow[:, : 3 * part_width].reshape(shard, 3, part_width)
+    grad_out = narrow[:, 3 * part_width :].T
+    n_vec = 6 * (width // 2 // n_dp)
+    n_bias = 3 * (part_width // n_dp)
+    grad_vectors = tiny[:n_vec].reshape(6, -1)
+    grad_bqkv = tiny[n_vec : n_vec + n_bias].reshape(3, -1)
+    grad_bup = tiny[n_vec + n_bias :]
+    return (
+        section_outputs,
+        input_grads,
+        grad_qkv[None],
+        grad_bqkv[None],
+        grad_out[None],
+        grad_up[None],
+        grad_bup[None],
+        grad_down[None],
+        grad_vectors[None],
+    )
+
 
 HEAD = 64
 BLOCK = 64
@@ -462,8 +1463,13 @@
         P("section", "tensor", None),
         P("section", None, None),
     )
+    sizes = tuple(mesh.shape[axis] for axis in ALL_AXES)
+    if sizes[0] == 2 and sizes[1] == 2 and sizes[2] % 2 == 0:
+        body = functools.partial(chip_shards, sizes)
+    else:
+        body = shards
     return jax.shard_map(
-        shards,
+        body,
         mesh=mesh,
         in_specs=placed,
         out_specs=(

time: 1470 us -> 526 us (0.36)
  waiting for transfers between devices: 480 us -> 79.2 us
  matrix products: 396 us -> 0 us
  other arithmetic: 302 us -> 35.2 us
  Pallas kernels: 0 us -> 247 us
  local copies, waits for them, and re-layouts: 225 us -> 21.1 us
  starting transfers between devices: 12.4 us -> 131 us
  between operations: 22.4 us -> 2.3 us
  blocking collectives: 16.8 us -> 0 us
    dot_general x150 -> x0, matrix products: 382 us -> none  [the longest x96 167 us: split_dot(): jnp.einsum(form, left_piece, right_piece, preferred_element_type=single)]
    pallas_call x0 -> x14, Pallas kernels: none -> 247 us  [the longest x2 88.9 us: attn_backward(): pl.pallas_call(functools.partial(attn_backward_kernel, layer_no, n_heads)...]
    reduce_scatter x16 -> x0, waiting for transfers between devices: 228 us -> none  [the longest x3 58.3 us: layer_backward(): lax.psum_scatter(jnp.einsum('lce,dce->ld', row_block, qkv_mat, preferred_...]
    scatter-add x6 -> x0, other arithmetic: 195 us -> none  [place_blocks(): base_arr.at[index_rows].add(one_part)]
    all_gather x12 -> x0, waiting for transfers between devices: 160 us -> none  [the longest x3 55.7 us: layer_forward(): normed_all = lax.all_gather(normed, 'tensor', axis=0, tiled=True)]
    ppermute x4 -> x69, starting transfers between devices: 9.99 us -> 131 us  [send(): return lax.ppermute(value, ALL_AXES, pairs)]
    reduce_sum x41 -> x8, other arithmetic: 60.7 us -> 1.68 us  [the longest x2 1.55 us: chip_shards(): jnp.sum(vec_one, axis=1)]
    gather x22 -> x0, local copies, waits for them, and re-layouts: 55.5 us -> none  [the longest x16 51.1 us: pick_blocks(): one_table[index_rows]]
  transfers between devices with their start and end apart: 34 -> 69, of which waited for: 27 -> 15; matrix products, arithmetic and copies ran while one was open for 29% -> 10% of each run, Pallas kernels for 0% -> 42%
where the time goes in v1:
time: 526 us; the launch traced here: 516 us
  Pallas kernels  247 us (47%)
  starting transfers between devices  131 us (25%)
  waiting for transfers between devices  79.2 us (15%)
  other arithmetic  35.2 us (7%)
  local copies, waits for them, and re-layouts  21.1 us (4%)
    ppermute x69, starting transfers between devices, send(): return lax.ppermute(value, ALL_AXES, pairs)  131 us
    pallas_call x2, Pallas kernels, attn_backward(): pl.pallas_call(functools.partial(attn_backward_kernel, layer_no, n_heads)...  88.9 us
    ppermute x69, waiting for transfers between devices, send(): return lax.ppermute(value, ALL_AXES, pairs)  79.2 us
    pallas_call x2, Pallas kernels, attn_forward(): pl.pallas_call(functools.partial(attn_forward_kernel, layer_no, n_heads),...  75.8 us
    pallas_call x4, Pallas kernels, weight_grads(): pl.pallas_call(functools.partial(weight_grad_kernel, 2, n_first), grid=(n...  29.4 us
    pallas_call x2, Pallas kernels, ffn_forward(): pl.pallas_call(functools.partial(ffn_forward_kernel, layer_no, 3), grid=(...  23.6 us
    pallas_call x2, Pallas kernels, ffn_backward(): pl.pallas_call(functools.partial(ffn_backward_kernel, layer_no), grid=(se...  16.7 us
    pallas_call x2, Pallas kernels, norm_backward(): pl.pallas_call(functools.partial(norm_backward_kernel, layer_no), grid=(s...  12.5 us
  transfers between devices with their start and end apart: 69, of which 15 were waited for; matrix products, arithmetic and copies ran while one was open for 10% of the time, Pallas kernels for 42%

profile of v1, /device:TPU:0, one launch (start us, length us, event | category | flops | bytes accessed | tf_op | source)
XLA Modules:
  0.0 515.7 jit_solution(15344653167995373540)
XLA Ops:
  11.7 25.0 %collective-permute-done.1.refs_2_.refs_4_.refs_7_.refs_10_.refs_1_ = bf16[16,1024]{1,0:T(8,128)(2,1)S(1)} collective-permute-done((bf16[16,1024]{1,0:T(8,128)(2,1)S(1)}, bf16[16,1024]{1,0:T(8,128)(2,1)S(1)}, u32[]{:S(2)}, u32[]{:S(2)}) %collective-permute-start.1) | collective-permute-done | bytes 32800 | tf_op jit(solution)/shard_map/ppermute | solution.py:779
  36.7 8.9 %collective-permute-start.2 = (bf16[16,1024]{1,0:T(8,128)(2,1)S(1)}, bf16[16,1024]{1,0:T(8,128)(2,1)S(1)}, u32[]{:S(2)}, u32[]{:S(2)}) collective-permute-start(bf16[16,1024]{1,0:T(8,128)(2,1)S(1)} %collective-permute-done.1.refs_2_.refs_4_.refs_7_.refs_10_.refs_1_), channel_id=1, source_target_pairs={{0,8},{2,10},{4,12},{6,14},{9,1},{11,3},{13,5},{15,7},{16,24},{18,... | collective-permute-start | bytes 98312 | tf_op jit(solution)/shard_map/ppermute | solution.py:779
  61.8 7.9 %collective-permute-start.13 = (bf16[512,1024]{1,0:T(8,128)(2,1)S(1)}, bf16[512,1024]{1,0:T(8,128)(2,1)S(1)}, u32[]{:S(2)}, u32[]{:S(2)}) collective-permute-start(bf16[512,1024]{1,0:T(8,128)(2,1)S(1)} %collective-permute-done.12.refs_7_.refs_1_), channel_id=1, source_target_pairs={{0,8},{2,10},{4,12},{6,14},{9,1},{11,3},{13,5},{15,7},{16,24},{18,... | collective-permute-start | bytes 3145736 | tf_op jit(solution)/shard_map/ppermute | solution.py:779
  74.5 37.2 %attn_forward_0.1 = (bf16[1024,512]{1,0:T(8,128)(2,1)}, bf16[3,1024,256]{2,1,0:T(8,128)(2,1)}, bf16[1024,512]{1,0:T(8,128)(2,1)}, bf16[4,1024,256]{2,1,0:T(8,128...) custom-call(s32[1]{0:T(128)} %bitcast.length_ref, ...), custom_call_target="tpu_custom_call" | custom-call | flops 4000000000 | bytes 16777216 | tf_op jit(solution)/shard_map/attn_forward_0/pallas_call | solution.py:293
  114.8 11.8 %ffn_forward_0.1 = (bf16[1024,512]{1,0:T(8,128)(2,1)}, f32[1024,512]{1,0:T(8,128)}, bf16[1024,512]{1,0:T(8,128)(2,1)}, bf16[1024,1024]{1,0:T(8,128)(2,1)}, bf16[1024,1024]{1,0:T(8,128)(2,1)}) custom-call(bf16[1024,512]{1,0:T(8,128)(2,1)} %pad_maximum_fusion.refs_0_.x_ref, bf16[1024,512]{1,0:T(8,128)(2,1)} %get-tuple-element.58.refs_1_, ...), custom_call_target="tpu_custom_call" | custom-call | flops 2147483648 | bytes 14680064 | tf_op jit(solution)/shard_map/ffn_forward_0/pallas_call | solution.py:364
  130.5 38.7 %attn_forward_1.1 = (bf16[1024,512]{1,0:T(8,128)(2,1)}, bf16[1024,512]{1,0:T(8,128)(2,1)}, bf16[3,1024,256]{2,1,0:T(8,128)(2,1)}, bf16[1024,512]{1,0:T(8,128)(2,...) custom-call(s32[1]{0:T(128)} %bitcast.length_ref, ...), custom_call_target="tpu_custom_call" | custom-call | flops 4000000000 | bytes 16777216 | tf_op jit(solution)/shard_map/attn_forward_1/pallas_call | solution.py:293
  175.3 11.8 %ffn_forward_1.1 = (bf16[1024,512]{1,0:T(8,128)(2,1)}, f32[1024,512]{1,0:T(8,128)}, bf16[1024,512]{1,0:T(8,128)(2,1)}, bf16[1024,1024]{1,0:T(8,128)(2,1)}, bf16[1024,1024]{1,0:T(8,128)(2,1)}) custom-call(bf16[1024,512]{1,0:T(8,128)(2,1)} %get-tuple-element.61.refs_0_.x_ref, bf16[1024,512]{1,0:T(8,128)(2,1)} %get-tuple-element.62.refs_1_, ...), custom_call_target="tpu_custom_call" | custom-call | flops 2147483648 | bytes 14680064 | tf_op jit(solution)/shard_map/ffn_forward_1/pallas_call | solution.py:364
  187.2 8.4 %ffn_backward_1.1 = (bf16[1024,512]{1,0:T(8,128)(2,1)}, bf16[1024,1024]{1,0:T(8,128)(2,1)}, f32[8,1024]{1,0:T(8,128)}) custom-call(bf16[1024,512]{1,0:T(8,128)(2,1)} %pad_maximum_fusion.1.grad_ref.refs_0_.left_b, bf16[1024,1024]{1,0:T(8,128)(2,1)} %get-tuple-element.65.slope_ref, bf16[512,1024]{1,0:T(8,128)(2,1)} %bitcast.136, bf16[512,1024]{1,0:T(8,128)(2,1)} %copy-done, ...), custom_call_target="tpu_custom_call" | custom-call | flops 2147483648 | bytes 8388608 | tf_op jit(solution)/shard_map/ffn_backward_1/pallas_call | solution.py:429
  199.0 44.5 %attn_backward_1.1 = (bf16[1024,512]{1,0:T(8,128)(2,1)}, f32[1024,512]{1,0:T(8,128)}, bf16[1024,512]{1,0:T(8,128)(2,1)}, bf16[3,1024,256]{2,1,0:T(8,128)(2,1)}, ...) custom-call(s32[192]{0:T(256)} %bitcast.167, bf16[1024,512]{1,0:T(8,128)(2,1)} %pad_maximum_fusion.1.grad_ref.refs_0_.left_b, ...), custom_call_target="tpu_custom_call" | custom-call | flops 8000000000 | bytes 20971520 | tf_op jit(solution)/shard_map/attn_backward_1/pallas_call | solution.py:626
  243.4 5.8 %attn_grads_1.1 = bf16[2,4,64,1024]{3,2,1,0:T(8,128)(2,1)} custom-call(bf16[1024,512]{1,0:T(8,128)(2,1)} %get-tuple-element.89.left_a, bf16[1024,512]{1,0:T(8,128)(2,1)} %get-tuple-element.90.left_b, bf16[3,1024,256]{2,1,0:T(8,128)(2,1)} %get-tuple-element.91.right_a, bf16[1024,256]{1,0:T(8,128)(2,1)} %get-tuple-element.92.right_b), custom_call_target="tpu_custom_call" | custom-call | flops 1073741824 | bytes 8388608 | tf_op jit(solution)/shard_map/attn_grads_1/pallas_call | solution.py:750
  252.3 5.4 %collective-permute-start.22 = (bf16[512,512]{1,0:T(8,128)(2,1)S(1)}, bf16[512,512]{1,0:T(8,128)(2,1)}, u32[]{:S(2)}, u32[]{:S(2)}) collective-permute-start(bf16[512,512]{1,0:T(8,128)(2,1)S(1)} %add_convert_fusion.8), channel_id=1, source_target_pairs={{0,16},{1,24},{2,18},{3,26},{4,20},{5,28},{6,22},{7,30},{8,17},{9,... | collective-permute-start | bytes 1572872 | tf_op jit(solution)/shard_map/ppermute | solution.py:779
  262.2 8.9 %ffn_grads_1.1 = bf16[2,4,64,2048]{3,2,1,0:T(8,128)(2,1)} custom-call(bf16[1024,512]{1,0:T(8,128)(2,1)} %get-tuple-element.104.left_a, bf16[1024,512]{1,0:T(8,128)(2,1)} %pad_maximum_fusion.1.grad_ref.refs_0_.left_b, bf16[1024,1024]{1,0:T(8,128)(2,1)} %get-tuple-element.105.right_a, bf16[1024,1024]{1,0:T(8,128)(2,1)} %get-tuple-element.106.right_b), custom_call_target="tpu_custom_call" | custom-call | flops 2147483648 | bytes 8388608 | tf_op jit(solution)/shard_map/ffn_grads_1/pallas_call | solution.py:750
  277.5 6.2 %norm_backward_1.1 = (f32[1024,512]{1,0:T(8,128)}, bf16[1024,512]{1,0:T(8,128)(2,1)}, f32[2,8,512]{2,1,0:T(8,128)}) custom-call(bf16[1024,512]{1,0:T(8,128)(2,1)} %get-tuple-element.61.refs_0_.x_ref, bf16[1024,512]{1,0:T(8,128)(2,1)} %get-tuple-element.72.part_a, bf16[1024,512]{1,0:T(8,128)(2,1)} %collective-permute-done.26.part_b, ...), custom_call_target="tpu_custom_call" | custom-call | flops 10485760 | bytes 8388608 | tf_op jit(solution)/shard_map/norm_backward_1/pallas_call | solution.py:694
  284.8 8.3 %ffn_backward_0.1 = (bf16[1024,512]{1,0:T(8,128)(2,1)}, bf16[1024,1024]{1,0:T(8,128)(2,1)}, f32[8,1024]{1,0:T(8,128)}) custom-call(bf16[1024,512]{1,0:T(8,128)(2,1)} %get-tuple-element.74.grad_ref.refs_0_.left_b, bf16[1024,1024]{1,0:T(8,128)(2,1)} %get-tuple-element.75.slope_ref, bf16[512,1024]{1,0:T(8,128)(2,1)} %bitcast.137, bf16[512,1024]{1,0:T(8,128)(2,1)} %copy-done, ...), custom_call_target="tpu_custom_call" | custom-call | flops 2147483648 | bytes 8388608 | tf_op jit(solution)/shard_map/ffn_backward_0/pallas_call | solution.py:429
  299.2 8.9 %ffn_grads_0.1 = bf16[2,4,64,2048]{3,2,1,0:T(8,128)(2,1)} custom-call(bf16[1024,512]{1,0:T(8,128)(2,1)} %get-tuple-element.101.left_a, bf16[1024,512]{1,0:T(8,128)(2,1)} %get-tuple-element.74.grad_ref.refs_0_.left_b, bf16[1024,1024]{1,0:T(8,128)(2,1)} %get-tuple-element.102.right_a, bf16[1024,1024]{1,0:T(8,128)(2,1)} %get-tuple-element.103.right_b), custom_call_target="tpu_custom_call" | custom-call | flops 2147483648 | bytes 8388608 | tf_op jit(solution)/shard_map/ffn_grads_0/pallas_call | solution.py:750
  315.7 44.4 %attn_backward_0.1 = (bf16[1024,512]{1,0:T(8,128)(2,1)}, f32[1024,512]{1,0:T(8,128)}, bf16[1024,512]{1,0:T(8,128)(2,1)}, bf16[3,1024,256]{2,1,0:T(8,128)(2,1)}, ...) custom-call(s32[192]{0:T(256)} %bitcast.165, bf16[1024,512]{1,0:T(8,128)(2,1)} %get-tuple-element.74.grad_ref.refs_0_.left_b, ...), custom_call_target="tpu_custom_call" | custom-call | flops 8000000000 | bytes 20971520 | tf_op jit(solution)/shard_map/attn_backward_0/pallas_call | solution.py:626
  360.1 3.0 collective-permute-start.28
  366.9 5.8 %attn_grads_0.1 = bf16[2,4,64,1024]{3,2,1,0:T(8,128)(2,1)} custom-call(bf16[1024,512]{1,0:T(8,128)(2,1)} %get-tuple-element.85.left_a, bf16[1024,512]{1,0:T(8,128)(2,1)} %get-tuple-element.86.left_b, bf16[3,1024,256]{2,1,0:T(8,128)(2,1)} %get-tuple-element.87.right_a, bf16[1024,256]{1,0:T(8,128)(2,1)} %get-tuple-element.88.right_b), custom_call_target="tpu_custom_call" | custom-call | flops 1073741824 | bytes 8388608 | tf_op jit(solution)/shard_map/attn_grads_0/pallas_call | solution.py:750
  374.3 5.2 %collective-permute-start.64 = (bf16[2,4,64,2048]{3,2,1,0:T(8,128)(2,1)S(1)}, bf16[2,4,64,2048]{3,2,1,0:T(8,128)(2,1)}, u32[]{:S(2)}, u32[]{:S(2)}) collective-permute-start(bf16[2,4,64,2048]{3,2,1,0:T(8,128)(2,1)S(1)} %add_convert_fusion.1), channel_id=1, source_target_pairs={{0,16},{2,18},{4,20},{6,22},{9,25},{11,27},{13,29},{15,31}} | collective-permute-start | bytes 6291464 | tf_op jit(solution)/shard_map/ppermute | solution.py:779
  380.4 6.3 %norm_backward_0.1 = (f32[1024,512]{1,0:T(8,128)}, bf16[1024,512]{1,0:T(8,128)(2,1)}, f32[2,8,512]{2,1,0:T(8,128)}) custom-call(bf16[1024,512]{1,0:T(8,128)(2,1)} %pad_maximum_fusion.refs_0_.x_ref, bf16[1024,512]{1,0:T(8,128)(2,1)} %get-tuple-element.82.part_a, bf16[1024,512]{1,0:T(8,128)(2,1)} %collective-permute-done.28.part_b, ...), custom_call_target="tpu_custom_call" | custom-call | flops 10485760 | bytes 8388608 | tf_op jit(solution)/shard_map/norm_backward_0/pallas_call | solution.py:694
  390.0 3.6 collective-permute-done.45
  402.9 3.7 add_convert_fusion.3
  408.6 4.5 collective-permute-start.49
  413.1 3.3 collective-permute-start.50
  423.4 5.4 %collective-permute-start.29 = (bf16[512,512]{1,0:T(8,128)(2,1)}, bf16[512,512]{1,0:T(8,128)(2,1)}, u32[]{:S(2)}, u32[]{:S(2)}) collective-permute-start(bf16[512,512]{1,0:T(8,128)(2,1)} %constant_dynamic-slice_fusion.13), channel_id=1, source_target_pairs={{0,0},{1,8},{2,2},{3,10},{4,4},{5,12},{6,6},{7,14},{8,1},{9,9},{10... | collective-permute-start | bytes 1572872 | tf_op jit(solution)/shard_map/ppermute | solution.py:779
  433.8 15.6 %collective-permute-done.31 = bf16[512,512]{1,0:T(8,128)(2,1)S(1)} collective-permute-done((bf16[512,512]{1,0:T(8,128)(2,1)}, bf16[512,512]{1,0:T(8,128)(2,1)S(1)}, u32[]{:S(2)}, u32[]{:S(2)}) %collective-permute-start.31) | collective-permute-done | bytes 524320 | tf_op jit(solution)/shard_map/ppermute | solution.py:779
  453.4 7.3 %collective-permute-done.34 = bf16[2,4,64,1024]{3,2,1,0:T(8,128)(2,1)S(1)} collective-permute-done((bf16[2,4,64,1024]{3,2,1,0:T(8,128)(2,1)S(1)}, bf16[2,4,64,1024]{3,2,1,0:T(8,128)(2,1)S(1)}, u32[]{:S(2)}, u32[]{:S(2)}) %collective-permute-start.34) | collective-permute-done | bytes 1048608 | tf_op jit(solution)/shard_map/ppermute | solution.py:779
  472.1 5.7 %collective-permute-start.38 = (bf16[64,1024]{1,0:T(8,128)(2,1)S(1)}, bf16[64,1024]{1,0:T(8,128)(2,1)S(1)}, u32[]{:S(2)}, u32[]{:S(2)}) collective-permute-start(bf16[64,1024]{1,0:T(8,128)(2,1)S(1)} %get-tuple-element.145), channel_id=1, source_target_pairs={{0,6},{1,7},{2,0},{3,1},{4,2},{5,3},{6,4},{7,5},{8,14},{9,15},{10,... | collective-permute-start | bytes 393224 | tf_op jit(solution)/shard_map/ppermute | solution.py:779
  483.9 3.9 collective-permute-start.60
  487.9 3.7 collective-permute-start.62
  497.2 4.4 collective-permute-done.62
  501.6 11.2 %collective-permute-done.61 = bf16[64,2048]{1,0:T(8,128)(2,1)} collective-permute-done((bf16[64,2048]{1,0:T(8,128)(2,1)}, bf16[64,2048]{1,0:T(8,128)(2,1)}, u32[]{:S(2)}, u32[]{:S(2)}) %collective-permute-start.61) | collective-permute-done | bytes 262176 | tf_op jit(solution)/shard_map/ppermute | solution.py:779
  (278 shorter events, 138.8 us)
Async XLA Ops:
  0.6 54.7 %collective-permute-start.5 = (bf16[3,512,256]{2,1,0:T(8,128)(2,1)}, bf16[3,512,256]{2,1,0:T(8,128)(2,1)}, u32[]{:S(2)}, u32[]{:S(2)}) collective-permute-start(bf16[3,512,256]{2,1,0:T(8,128)(2,1)} %bitcast.168), channel_id=1, source_target_pairs={{0,16},{1,8},{2,18},{3,10},{4,20},{5,12},{6,22},{7,14},{8,1},{9,25... | collective-permute-start | bytes 2359304 | tf_op jit(solution)/shard_map/ppermute | solution.py:779
  4.8 44.0 %collective-permute-start.3 = (bf16[512,512]{1,0:T(8,128)(2,1)S(1)}, bf16[512,512]{1,0:T(8,128)(2,1)S(1)}, u32[]{:S(2)}, u32[]{:S(2)}) collective-permute-start(bf16[512,512]{1,0:T(8,128)(2,1)S(1)} %dynamic-slice_bitcast_fusion.5), channel_id=1, source_target_pairs={{0,1},{1,9},{2,3},{3,11},{4,5},{5,13},{6,7},{7,15},{8,0},{9,8},{10... | collective-permute-start | bytes 1572872 | tf_op jit(solution)/shard_map/ppermute | solution.py:779
  4.9 56.9 %collective-permute-start.12 = (bf16[512,1024]{1,0:T(8,128)(2,1)}, bf16[512,1024]{1,0:T(8,128)(2,1)S(1)}, u32[]{:S(2)}, u32[]{:S(2)}) collective-permute-start(bf16[512,1024]{1,0:T(8,128)(2,1)} %bitcast.133), channel_id=1, source_target_pairs={{0,16},{1,8},{2,18},{3,10},{4,20},{5,12},{6,22},{7,14},{8,1},{9,25... | collective-permute-start | bytes 3145736 | tf_op jit(solution)/shard_map/ppermute | solution.py:779
  6.4 63.3 %collective-permute-start.14 = (bf16[1024,512]{1,0:T(8,128)(2,1)}, bf16[1024,512]{1,0:T(8,128)(2,1)S(1)}, u32[]{:S(2)}, u32[]{:S(2)}) collective-permute-start(bf16[1024,512]{1,0:T(8,128)(2,1)} %bitcast.138), channel_id=1, source_target_pairs={{0,16},{1,8},{2,18},{3,10},{4,20},{5,12},{6,22},{7,14},{8,1},{9,25... | collective-permute-start | bytes 3145736 | tf_op jit(solution)/shard_map/ppermute | solution.py:779
  10.5 26.2 %collective-permute-start.1 = (bf16[16,1024]{1,0:T(8,128)(2,1)S(1)}, bf16[16,1024]{1,0:T(8,128)(2,1)S(1)}, u32[]{:S(2)}, u32[]{:S(2)}) collective-permute-start(bf16[16,1024]{1,0:T(8,128)(2,1)S(1)} %concatenate.28.refs_1_.refs_3_.refs_6_.refs_9_.refs_0_), channel_id=1, source_target_pairs={{0,16},{1,8},{2,18},{3,10},{4,20},{5,12},{6,22},{7,14},{8,1},{9,25... | collective-permute-start | bytes 98312 | tf_op jit(solution)/shard_map/ppermute | solution.py:779
  55.3 19.2 %collective-permute-start.6 = (bf16[3,512,256]{2,1,0:T(8,128)(2,1)}, bf16[3,512,256]{2,1,0:T(8,128)(2,1)}, u32[]{:S(2)}, u32[]{:S(2)}) collective-permute-start(bf16[3,512,256]{2,1,0:T(8,128)(2,1)} %collective-permute-done.5.refs_5_.refs_10_.refs_13_), channel_id=1, source_target_pairs={{0,8},{2,10},{4,12},{6,14},{9,1},{11,3},{13,5},{15,7},{16,24},{18,... | collective-permute-start | bytes 2359304 | tf_op jit(solution)/shard_map/ppermute | solution.py:779
  61.8 50.0 %collective-permute-start.13 = (bf16[512,1024]{1,0:T(8,128)(2,1)S(1)}, bf16[512,1024]{1,0:T(8,128)(2,1)S(1)}, u32[]{:S(2)}, u32[]{:S(2)}) collective-permute-start(bf16[512,1024]{1,0:T(8,128)(2,1)S(1)} %collective-permute-done.12.refs_7_.refs_1_), channel_id=1, source_target_pairs={{0,8},{2,10},{4,12},{6,14},{9,1},{11,3},{13,5},{15,7},{16,24},{18,... | collective-permute-start | bytes 3145736 | tf_op jit(solution)/shard_map/ppermute | solution.py:779
  69.7 42.1 %collective-permute-start.15 = (bf16[1024,512]{1,0:T(8,128)(2,1)S(1)}, bf16[1024,512]{1,0:T(8,128)(2,1)}, u32[]{:S(2)}, u32[]{:S(2)}) collective-permute-start(bf16[1024,512]{1,0:T(8,128)(2,1)S(1)} %collective-permute-done.14.refs_10_.refs_4_), channel_id=1, source_target_pairs={{1,17},{3,19},{5,21},{7,23},{8,24},{10,26},{12,28},{14,30},{17,1},... | collective-permute-start | bytes 3145736 | tf_op jit(solution)/shard_map/ppermute | solution.py:779
  127.9 41.5 %collective-permute-start.23 = (bf16[512,512]{1,0:T(8,128)(2,1)S(1)}, bf16[512,512]{1,0:T(8,128)(2,1)S(1)}, u32[]{:S(2)}, u32[]{:S(2)}) collective-permute-start(bf16[512,512]{1,0:T(8,128)(2,1)S(1)} %dynamic-slice_bitcast_fusion.4), channel_id=1, source_target_pairs={{0,1},{1,9},{2,3},{3,11},{4,5},{5,13},{6,7},{7,15},{8,0},{9,8},{10... | collective-permute-start | bytes 1572872 | tf_op jit(solution)/shard_map/ppermute | solution.py:779
  196.0 54.6 %collective-permute-start.19 = (bf16[1024,512]{1,0:T(8,128)(2,1)S(1)}, bf16[1024,512]{1,0:T(8,128)(2,1)}, u32[]{:S(2)}, u32[]{:S(2)}) collective-permute-start(bf16[1024,512]{1,0:T(8,128)(2,1)S(1)} %copy-done.18), channel_id=1, source_target_pairs={{0,1},{1,0},{2,3},{3,2},{4,5},{5,4},{6,7},{7,6},{8,9},{9,8},{10,11... | collective-permute-start | bytes 3145736 | tf_op jit(solution)/shard_map/ppermute | solution.py:779
  196.2 62.9 %collective-permute-start.21 = (bf16[512,512]{1,0:T(8,128)(2,1)S(1)}, bf16[512,512]{1,0:T(8,128)(2,1)S(1)}, u32[]{:S(2)}, u32[]{:S(2)}) collective-permute-start(bf16[512,512]{1,0:T(8,128)(2,1)S(1)} %constant_dynamic-slice_fusion.14), channel_id=1, source_target_pairs={{16,0},{17,8},{18,2},{19,10},{20,4},{21,12},{22,6},{23,14},{24,1},... | collective-permute-start | bytes 1572872 | tf_op jit(solution)/shard_map/ppermute | solution.py:779
  197.5 73.8 %collective-permute-start.17 = (bf16[512,512]{1,0:T(8,128)(2,1)S(1)}, bf16[512,512]{1,0:T(8,128)(2,1)}, u32[]{:S(2)}, u32[]{:S(2)}) collective-permute-start(bf16[512,512]{1,0:T(8,128)(2,1)S(1)} %constant_dynamic-slice_fusion.14), channel_id=1, source_target_pairs={{0,0},{1,8},{2,2},{3,10},{4,4},{5,12},{6,6},{7,14},{8,1},{9,9},{10... | collective-permute-start | bytes 1572872 | tf_op jit(solution)/shard_map/ppermute | solution.py:779
  249.3 24.9 %collective-permute-start.39 = (bf16[2,4,64,1024]{3,2,1,0:T(8,128)(2,1)}, bf16[2,4,64,1024]{3,2,1,0:T(8,128)(2,1)S(1)}, u32[]{:S(2)}, u32[]{:S(2)}) collective-permute-start(bf16[2,4,64,1024]{3,2,1,0:T(8,128)(2,1)} %attn_grads_1.1), channel_id=1, source_target_pairs={{1,9},{3,11},{5,13},{7,15},{8,0},{10,2},{12,4},{14,6},{17,25},{19,... | collective-permute-start | bytes 3145736 | tf_op jit(solution)/shard_map/ppermute | solution.py:779
  252.3 20.5 %collective-permute-start.22 = (bf16[512,512]{1,0:T(8,128)(2,1)S(1)}, bf16[512,512]{1,0:T(8,128)(2,1)}, u32[]{:S(2)}, u32[]{:S(2)}) collective-permute-start(bf16[512,512]{1,0:T(8,128)(2,1)S(1)} %add_convert_fusion.8), channel_id=1, source_target_pairs={{0,16},{1,24},{2,18},{3,26},{4,20},{5,28},{6,22},{7,30},{8,17},{9,... | collective-permute-start | bytes 1572872 | tf_op jit(solution)/shard_map/ppermute | solution.py:779
  271.3 88.8 %collective-permute-start.63 = (bf16[2,4,64,2048]{3,2,1,0:T(8,128)(2,1)}, bf16[2,4,64,2048]{3,2,1,0:T(8,128)(2,1)}, u32[]{:S(2)}, u32[]{:S(2)}) collective-permute-start(bf16[2,4,64,2048]{3,2,1,0:T(8,128)(2,1)} %ffn_grads_1.1), channel_id=1, source_target_pairs={{1,9},{3,11},{5,13},{7,15},{8,0},{10,2},{12,4},{14,6},{17,25},{19,... | collective-permute-start | bytes 6291464 | tf_op jit(solution)/shard_map/ppermute | solution.py:779
  274.6 34.9 %collective-permute-start.40 = (bf16[2,4,64,1024]{3,2,1,0:T(8,128)(2,1)S(1)}, bf16[2,4,64,1024]{3,2,1,0:T(8,128)(2,1)S(1)}, u32[]{:S(2)}, u32[]{:S(2)}) collective-permute-start(bf16[2,4,64,1024]{3,2,1,0:T(8,128)(2,1)S(1)} %add_convert_fusion.5), channel_id=1, source_target_pairs={{0,16},{2,18},{4,20},{6,22},{9,25},{11,27},{13,29},{15,31}} | collective-permute-start | bytes 3145736 | tf_op jit(solution)/shard_map/ppermute | solution.py:779
  293.1 21.1 %collective-permute-start.27 = (bf16[1024,512]{1,0:T(8,128)(2,1)}, bf16[1024,512]{1,0:T(8,128)(2,1)}, u32[]{:S(2)}, u32[]{:S(2)}) collective-permute-start(bf16[1024,512]{1,0:T(8,128)(2,1)} %get-tuple-element.76.refs_1_), channel_id=1, source_target_pairs={{0,1},{1,0},{2,3},{3,2},{4,5},{5,4},{6,7},{7,6},{8,9},{9,8},{10,11... | collective-permute-start | bytes 3145736 | tf_op jit(solution)/shard_map/ppermute | solution.py:779
  296.8 111.1 %collective-permute-start.32 = (bf16[512,512]{1,0:T(8,128)(2,1)}, bf16[512,512]{1,0:T(8,128)(2,1)}, u32[]{:S(2)}, u32[]{:S(2)}) collective-permute-start(bf16[512,512]{1,0:T(8,128)(2,1)} %constant_dynamic-slice_fusion.12), channel_id=1, source_target_pairs={{0,16},{1,24},{2,18},{3,26},{4,20},{5,28},{6,22},{7,30},{8,17},{9,... | collective-permute-start | bytes 1572872 | tf_op jit(solution)/shard_map/ppermute | solution.py:779
  308.1 94.8 %collective-permute-start.57 = (bf16[2,4,64,2048]{3,2,1,0:T(8,128)(2,1)}, bf16[2,4,64,2048]{3,2,1,0:T(8,128)(2,1)}, u32[]{:S(2)}, u32[]{:S(2)}) collective-permute-start(bf16[2,4,64,2048]{3,2,1,0:T(8,128)(2,1)} %ffn_grads_0.1), channel_id=1, source_target_pairs={{1,9},{3,11},{5,13},{7,15},{8,0},{10,2},{12,4},{14,6},{17,25},{19,... | collective-permute-start | bytes 6291464 | tf_op jit(solution)/shard_map/ppermute | solution.py:779
  310.4 55.7 %collective-permute-start.52 = (f32[2,4,416]{2,1,0:T(4,128)S(1)}, f32[2,4,416]{2,1,0:T(4,128)S(1)}, u32[]{:S(2)}, u32[]{:S(2)}) collective-permute-start(f32[2,4,416]{2,1,0:T(4,128)S(1)} %fusion.19), channel_id=1, source_target_pairs={{0,16},{2,18},{4,20},{6,22},{9,25},{11,27},{13,29},{15,31}} | collective-permute-start | bytes 39944 | tf_op jit(solution)/shard_map/ppermute | solution.py:779
  314.2 60.1 %collective-permute-start.41 = (bf16[4,64,1024]{2,1,0:T(8,128)(2,1)}, bf16[4,64,1024]{2,1,0:T(8,128)(2,1)}, u32[]{:S(2)}, u32[]{:S(2)}) collective-permute-start(bf16[4,64,1024]{2,1,0:T(8,128)(2,1)} %dynamic-slice_bitcast_fusion.2), channel_id=1, source_target_pairs={{16,17},{18,19},{20,21},{22,23},{25,24},{27,26},{29,28},{31,30}} | collective-permute-start | bytes 1572872 | tf_op jit(solution)/shard_map/ppermute | solution.py:779
  360.1 20.2 %collective-permute-start.28 = (bf16[1024,512]{1,0:T(8,128)(2,1)}, bf16[1024,512]{1,0:T(8,128)(2,1)}, u32[]{:S(2)}, u32[]{:S(2)}) collective-permute-start(bf16[1024,512]{1,0:T(8,128)(2,1)} %get-tuple-element.82.part_a), channel_id=1, source_target_pairs={{0,1},{1,0},{2,3},{3,2},{4,5},{5,4},{6,7},{7,6},{8,9},{9,8},{10,11... | collective-permute-start | bytes 3145736 | tf_op jit(solution)/shard_map/ppermute | solution.py:779
  372.8 22.5 %collective-permute-start.33 = (bf16[2,4,64,1024]{3,2,1,0:T(8,128)(2,1)}, bf16[2,4,64,1024]{3,2,1,0:T(8,128)(2,1)}, u32[]{:S(2)}, u32[]{:S(2)}) collective-permute-start(bf16[2,4,64,1024]{3,2,1,0:T(8,128)(2,1)} %attn_grads_0.1), channel_id=1, source_target_pairs={{1,9},{3,11},{5,13},{7,15},{8,0},{10,2},{12,4},{14,6},{17,25},{19,... | collective-permute-start | bytes 3145736 | tf_op jit(solution)/shard_map/ppermute | solution.py:779
  374.3 34.3 %collective-permute-start.64 = (bf16[2,4,64,2048]{3,2,1,0:T(8,128)(2,1)S(1)}, bf16[2,4,64,2048]{3,2,1,0:T(8,128)(2,1)}, u32[]{:S(2)}, u32[]{:S(2)}) collective-permute-start(bf16[2,4,64,2048]{3,2,1,0:T(8,128)(2,1)S(1)} %add_convert_fusion.1), channel_id=1, source_target_pairs={{0,16},{2,18},{4,20},{6,22},{9,25},{11,27},{13,29},{15,31}} | collective-permute-start | bytes 6291464 | tf_op jit(solution)/shard_map/ppermute | solution.py:779
  406.6 55.2 %collective-permute-start.58 = (bf16[2,4,64,2048]{3,2,1,0:T(8,128)(2,1)}, bf16[2,4,64,2048]{3,2,1,0:T(8,128)(2,1)}, u32[]{:S(2)}, u32[]{:S(2)}) collective-permute-start(bf16[2,4,64,2048]{3,2,1,0:T(8,128)(2,1)} %add_convert_fusion.3), channel_id=1, source_target_pairs={{16,0},{18,2},{20,4},{22,6},{25,9},{27,11},{29,13},{31,15}} | collective-permute-start | bytes 6291464 | tf_op jit(solution)/shard_map/ppermute | solution.py:779
  422.1 27.3 %collective-permute-start.31 = (bf16[512,512]{1,0:T(8,128)(2,1)}, bf16[512,512]{1,0:T(8,128)(2,1)S(1)}, u32[]{:S(2)}, u32[]{:S(2)}) collective-permute-start(bf16[512,512]{1,0:T(8,128)(2,1)} %constant_dynamic-slice_fusion.13), channel_id=1, source_target_pairs={{16,0},{17,8},{18,2},{19,10},{20,4},{21,12},{22,6},{23,14},{24,1},... | collective-permute-start | bytes 1572872 | tf_op jit(solution)/shard_map/ppermute | solution.py:779
  423.4 26.6 %collective-permute-start.29 = (bf16[512,512]{1,0:T(8,128)(2,1)}, bf16[512,512]{1,0:T(8,128)(2,1)}, u32[]{:S(2)}, u32[]{:S(2)}) collective-permute-start(bf16[512,512]{1,0:T(8,128)(2,1)} %constant_dynamic-slice_fusion.13), channel_id=1, source_target_pairs={{0,0},{1,8},{2,2},{3,10},{4,4},{5,12},{6,6},{7,14},{8,1},{9,9},{10... | collective-permute-start | bytes 1572872 | tf_op jit(solution)/shard_map/ppermute | solution.py:779
  428.8 31.9 %collective-permute-start.34 = (bf16[2,4,64,1024]{3,2,1,0:T(8,128)(2,1)S(1)}, bf16[2,4,64,1024]{3,2,1,0:T(8,128)(2,1)S(1)}, u32[]{:S(2)}, u32[]{:S(2)}) collective-permute-start(bf16[2,4,64,1024]{3,2,1,0:T(8,128)(2,1)S(1)} %add_convert_fusion.7), channel_id=1, source_target_pairs={{16,0},{18,2},{20,4},{22,6},{25,9},{27,11},{29,13},{31,15}} | collective-permute-start | bytes 3145736 | tf_op jit(solution)/shard_map/ppermute | solution.py:779
  433.1 38.9 %collective-permute-start.42 = (bf16[64,1024]{1,0:T(8,128)(2,1)}, bf16[64,1024]{1,0:T(8,128)(2,1)S(1)}, u32[]{:S(2)}, u32[]{:S(2)}) collective-permute-start(bf16[64,1024]{1,0:T(8,128)(2,1)} %get-tuple-element.147), channel_id=1, source_target_pairs={{16,18},{17,19},{18,20},{19,21},{20,22},{21,23},{22,16},{23,17},{2... | collective-permute-start | bytes 393224 | tf_op jit(solution)/shard_map/ppermute | solution.py:779
  449.4 28.4 %collective-permute-start.44 = (bf16[64,1024]{1,0:T(8,128)(2,1)}, bf16[64,1024]{1,0:T(8,128)(2,1)S(1)}, u32[]{:S(2)}, u32[]{:S(2)}) collective-permute-start(bf16[64,1024]{1,0:T(8,128)(2,1)} %get-tuple-element.148), channel_id=1, source_target_pairs={{16,22},{17,23},{18,16},{19,17},{20,18},{21,19},{22,20},{23,21},{2... | collective-permute-start | bytes 393224 | tf_op jit(solution)/shard_map/ppermute | solution.py:779
  450.1 31.2 %collective-permute-start.43 = (bf16[64,1024]{1,0:T(8,128)(2,1)S(1)}, bf16[64,1024]{1,0:T(8,128)(2,1)S(1)}, u32[]{:S(2)}, u32[]{:S(2)}) collective-permute-start(bf16[64,1024]{1,0:T(8,128)(2,1)S(1)} %get-tuple-element.149), channel_id=1, source_target_pairs={{16,20},{17,21},{18,22},{19,23},{20,16},{21,17},{22,18},{23,19},{2... | collective-permute-start | bytes 393224 | tf_op jit(solution)/shard_map/ppermute | solution.py:779
  491.6 21.2 %collective-permute-start.61 = (bf16[64,2048]{1,0:T(8,128)(2,1)}, bf16[64,2048]{1,0:T(8,128)(2,1)}, u32[]{:S(2)}, u32[]{:S(2)}) collective-permute-start(bf16[64,2048]{1,0:T(8,128)(2,1)} %get-tuple-element.138), channel_id=1, source_target_pairs={{0,4},{1,5},{2,6},{3,7},{4,0},{5,1},{6,2},{7,3},{8,12},{9,13},{10,... | collective-permute-start | bytes 786440 | tf_op jit(solution)/shard_map/ppermute | solution.py:779
  (68 other events, 735.4 us)
